TPU v7x, 32 devices: a whole 2x2x4 slice. The times are simulated.
32 devices in a mesh: teacher: 4 (over y, core), seq: 8 (over z, x).
Axes of the slice: x: 2, y: 2, z: 4, core: 2. Of those that a mesh axis runs over, the one named last changes fastest.
Arguments:
- activations: bfloat16 [20, 512, 1536], P('teacher', 'seq'), may hold values from -150 to 150
- teacher_maps: bfloat16 [4, 20, 512, 1536], P('teacher', None, 'seq'), may hold values from -6 to 6
- projection: bfloat16 [4, 1536, 1536], P('teacher', 'seq'), may hold values from -0.4375 to 0.4375
- dilated_weight: bfloat16 [1536, 3, 768], P('seq'), may hold values from -0.09375 to 0.09375
- pointwise_weight: bfloat16 [768, 1536], P('seq'), may hold values from -0.21875 to 0.21875
Outputs:
- loss_mean: float32 [], replicated
- dilated_grad: float32 [1536, 3, 768], P('seq')
- pointwise_grad: float32 [768, 1536], P('seq')
All inputs are finite; a program needn't handle non-finite values.
Results may differ from a plain program's by a relative error of at most 0.00081.
Values may be sent and summed in bfloat16 or wider, within the bound.
A program may use at most 128 MiB of HBM per device.

v0:
```python
import jax
import jax.numpy as jnp
from jax import lax
from jax.sharding import PartitionSpec as P

TAP_DILATION = 16


slope_const = 0.7978845608
cubic_const = 0.044715


def padded(block, sides, width):
    for axis, dim in sides:
        count = lax.axis_size(axis)
        forward = [(i, i + 1) for i in range(count - 1)]
        backward = [(target, source) for source, target in forward]
        low = lax.ppermute(
            lax.slice_in_dim(block, block.shape[dim] - width, None, axis=dim), axis, forward
        )
        high = lax.ppermute(lax.slice_in_dim(block, 0, width, axis=dim), axis, backward)
        block = jnp.concatenate([low, block, high], axis=dim)
    return block


def gelu_tanh(value):
    inside = slope_const * (value + cubic_const * value * value * value)
    return 0.5 * value * (1.0 + jnp.tanh(inside))


def gelu_slope(value):
    inside = slope_const * (value + cubic_const * value * value * value)
    tangent = jnp.tanh(inside)
    return 0.5 * (1.0 + tangent) + 0.5 * value * (1.0 - tangent * tangent) * slope_const * (
        1.0 + 3.0 * cubic_const * value * value
    )


def column_product(left, right):
    return lax.dot_general(
        left, right, (((0,), (0,)), ((), ())), preferred_element_type=jnp.float32
    )


def shards(activations, teacher_maps, projection, dilated_weight, pointwise_weight):
    groups = lax.axis_size("teacher")
    ranks = lax.axis_size("seq")
    win_grp, bins_per_device, channel_count = activations.shape
    branch_width = dilated_weight.shape[2]
    count_of_rows = win_grp * bins_per_device
    total_rows = count_of_rows * groups * ranks
    maps_flat = teacher_maps[0].reshape(-1, teacher_maps.shape[3])
    columns = maps_flat
    projected = jnp.dot(
        columns,
        lax.all_gather(projection, "seq", axis=1, tiled=True)[0],
        preferred_element_type=jnp.float32,
    )
    projected = lax.optimization_barrier(projected.astype(jnp.bfloat16)).astype(jnp.float32)
    summed = lax.psum(projected, "teacher")
    own_rows = lax.dynamic_slice_in_dim(
        summed, lax.axis_index("teacher") * count_of_rows, count_of_rows, 0
    )
    target = own_rows / groups
    inputs_f = activations.reshape(count_of_rows, channel_count).astype(jnp.float32)
    sum_first, sum_second = lax.psum(
        (jnp.sum(inputs_f, axis=0), jnp.sum(inputs_f * inputs_f, axis=0)), ("teacher", "seq")
    )
    channel_mean = sum_first / total_rows
    channel_var = sum_second / total_rows - channel_mean * channel_mean
    normed = (inputs_f - channel_mean) * lax.rsqrt(channel_var + 1e-05)
    hidden_state = (
        gelu_tanh(normed).astype(jnp.bfloat16).reshape(win_grp, bins_per_device, channel_count)
    )
    padded_input = padded(hidden_state, (("seq", 1),), TAP_DILATION)
    tap_weights = [
        padded_input[
            :, offset_index * TAP_DILATION : offset_index * TAP_DILATION + bins_per_device
        ].reshape(count_of_rows, channel_count)
        for offset_index in range(3)
    ]
    running = jnp.zeros((count_of_rows, branch_width), jnp.float32)
    section = lax.all_gather(dilated_weight, "seq", axis=0, tiled=True)
    for add_offset_index in range(3):
        columns = tap_weights[add_offset_index]
        running = running + jnp.dot(
            columns, section[:, add_offset_index, :], preferred_element_type=jnp.float32
        )
    activated = gelu_tanh(running).astype(jnp.bfloat16)
    pointwise_full = lax.all_gather(pointwise_weight, "seq", axis=0, tiled=True)
    student = inputs_f + jnp.dot(activated, pointwise_full, preferred_element_type=jnp.float32)
    misfit = student - target
    squared_total = lax.psum(jnp.sum(misfit * misfit), ("teacher", "seq"))
    loss_mean = 0.5 * squared_total / (channel_count * total_rows)
    out_grad = (misfit / channel_count).astype(jnp.bfloat16)
    back_grad = lax.dot_general(
        out_grad, pointwise_full, (((1,), (1,)), ((), ())), preferred_element_type=jnp.float32
    )
    preact_grad = (back_grad * gelu_slope(running)).astype(jnp.bfloat16)

    def regroup_columns(matrix):
        return (
            matrix.reshape(count_of_rows, ranks, groups, -1)
            .transpose(0, 2, 1, 3)
            .reshape(count_of_rows, -1)
        )

    taps_moved = [regroup_columns(tap_weights[offset_index]) for offset_index in range(3)]
    activated_moved = regroup_columns(activated)
    dilated_share = lax.psum_scatter(
        jnp.stack(
            [column_product(taps_moved[offset_index], preact_grad) for offset_index in range(3)],
            axis=1,
        ),
        ("teacher", "seq"),
        scatter_dimension=0,
        tiled=True,
    )
    pointwise_share = lax.psum_scatter(
        column_product(activated_moved, out_grad),
        ("teacher", "seq"),
        scatter_dimension=0,
        tiled=True,
    )
    dilated_grad, pointwise_grad = (
        lax.all_gather(dilated_share, "teacher", axis=0, tiled=True),
        lax.all_gather(pointwise_share, "teacher", axis=0, tiled=True),
    )
    return (loss_mean, dilated_grad, pointwise_grad)


def solution(mesh):
    in_specs = (
        P("teacher", "seq", None),
        P("teacher", None, "seq", None),
        P("teacher", "seq", None),
        P("seq", None, None),
        P("seq", None),
    )
    out_specs = (P(), P("seq", None, None), P("seq", None))
    return jax.shard_map(shards, mesh=mesh, in_specs=in_specs, out_specs=out_specs, check_vma=False)
```

profile of v0, /device:TPU:11, one launch (start us, length us, event | category | flops | bytes accessed | tf_op | source)
XLA Modules:
  0.0 599.7 jit_solution(13248696465132320495)
XLA Ops:
  10.2 41.2 %all-reduce = (f32[1536]{0:T(1024)S(1)}, f32[1536]{0:T(1024)S(1)}) all-reduce(f32[1536]{0:T(1024)S(1)} %get-tuple-element.4, f32[1536]{0:T(1024)S(1)} %get-tuple-element.3), channel_id=1, replica_groups=mesh['teacher'=4,'seq'=8] {'teacher','seq'}, use_global_device_ids=true, to_apply=%region_3.0 | all-reduce | flops 3072 | bytes 24576 | tf_op jit(solution)/shard_map/psum | solution.py:66
  53.2 3.5 collective-permute-start
  59.3 7.2 %reshape.71 = f32[320,8,4,48]{3,2,1,0:T(4,128)} reshape(bf16[5,64,1536]{2,1,0:T(8,128)(2,1)S(1)} %copy-done) | data formatting | bytes 2949120 | tf_op jit(solution)/shard_map/convert_element_type | solution.py:65
  66.4 6.5 %copy.14 = f32[320,8,4,48]{0,3,2,1:T(8,128)} copy(f32[320,8,4,48]{3,2,1,0:T(4,128)} %reshape.71) | data formatting | bytes 3932160 | tf_op jit(solution)/shard_map/convert_element_type | solution.py:65
  79.2 7.2 %reshape_reshape.6 = bf16[320,8,4,48]{3,2,1,0:T(4,128)(2,1)} reshape(bf16[5,64,1536]{2,1,0:T(8,128)(2,1)} %get-tuple-element.7) | data formatting | bytes 1966080 | tf_op jit(solution)/shard_map/reshape;reshape | solution.py:103
  86.4 5.8 copy.13
  92.2 7.2 %reshape_reshape.7 = bf16[320,8,4,48]{3,2,1,0:T(4,128)(2,1)} reshape(bf16[5,64,1536]{2,1,0:T(8,128)(2,1)} %get-tuple-element.8) | data formatting | bytes 1966080 | tf_op jit(solution)/shard_map/reshape;reshape | solution.py:103
  99.4 5.8 copy.16
  105.1 10.7 %convolution_convert_fusion = bf16[1280,1536]{1,0:T(8,128)(2,1)} fusion(bf16[1280,1536]{1,0:T(8,128)(2,1)} %bitcast.65, bf16[1,1536,1536]{2,1,0:T(8,128)(2,1)} %all-gather.9.cloned.1.call-done), kind=kOutput, calls=%fused_computation.1 | convolution fusion | flops 6041763840 | bytes 12582912 | tf_op jit(solution)/shard_map/dot_general | solution.py:54
  115.8 140.8 %all-reduce.2 = f32[1280,1536]{1,0:T(8,128)} all-reduce(bf16[1280,1536]{1,0:T(8,128)(2,1)} %convolution_convert_fusion), channel_id=1, replica_groups=mesh['teacher'=4,'seq'=8] {'teacher'}, use_global_device_ids=true, to_apply=%region_4.0 | all-reduce | flops 1966080 | bytes 11796480 | tf_op jit(solution)/shard_map/psum | solution.py:60
  256.7 2.7 fusion.8
  262.1 2.8 multiply_convert_fusion.1
  264.9 4.1 multiply_reduce_fusion
  270.9 3.5 convolution_bitcast_fusion
  274.4 3.6 convolution_bitcast_fusion.2
  278.0 3.6 convolution_bitcast_fusion.1
  281.6 11.1 %pad_maximum_fusion = f32[1536,3,768]{2,0,1:T(8,128)} fusion(f32[1536,1,768]{2,0,1:T(8,128)} %convolution_bitcast_fusion, f32[1536,1,768]{2,0,1:T(8,128)} %convolution_bitcast_fusion.1, f32[1536,1,768]{2,0,1:T(8,128)} %convolution_bitcast_fusion.2), kind=kLoop, calls=%fused_computation | loop fusion | flops 7077888 | bytes 28311552 | tf_op jit(solution)/shard_map/stack | solution.py:111
  294.3 3.5 fusion.24
  297.9 155.2 %reduce-scatter.3.cloned.1.call-done = f32[48,3,768]{2,0,1:T(8,128)} async-done(((f32[1536,3,768]{2,0,1:T(8,128)}), f32[48,3,768]{2,0,1:T(8,128)}) %reduce-scatter.3.cloned.1.call-update) | async-done | bytes 442384 | tf_op jit(solution)/shard_map/reduce_scatter | solution.py:110
  453.1 40.8 %psum.31 = f32[]{:T(128)} all-reduce(f32[]{:T(128)} %get-tuple-element.15), channel_id=1, replica_groups=mesh['teacher'=4,'seq'=8] {'teacher','seq'}, use_global_device_ids=true, to_apply=%region_6.0 | all-reduce | flops 1 | bytes 8 | tf_op jit(solution)/shard_map/psum | solution.py:93
  494.5 70.1 %reduce-scatter.5.cloned.1.call-done = f32[24,1536]{1,0:T(8,128)} async-done(((f32[768,1536]{1,0:T(8,128)}), f32[24,1536]{1,0:T(8,128)}) %reduce-scatter.5.cloned.1.call-update) | async-done | bytes 147472 | tf_op jit(solution)/shard_map/reduce_scatter | solution.py:119
  564.6 9.8 %all_gather.19 = f32[96,1536]{1,0:T(8,128)S(1)} all-gather(f32[24,1536]{1,0:T(8,128)} %reduce-scatter.5.cloned.1.call-done), channel_id=1, replica_groups=mesh['teacher'=4,'seq'=8] {'teacher'}, dimensions={0}, use_global_device_ids=true | all-gather | bytes 737280 | tf_op jit(solution)/shard_map/all_gather | solution.py:127
  574.4 13.7 %all-gather.11.cloned.1.call-done = f32[192,3,768]{2,0,1:T(8,128)} async-done(((f32[48,3,768]{2,0,1:T(8,128)}), f32[192,3,768]{2,0,1:T(8,128)}) %all-gather.11.cloned.1.call-update) | async-done | bytes 1769488 | tf_op jit(solution)/shard_map/all_gather | solution.py:126
  588.1 2.8 copy.23
  (55 shorter events, 20.6 us)
Async XLA Ops:
  7.2 44.2 %copy-start = (bf16[5,64,1536]{2,1,0:T(8,128)(2,1)S(1)}, bf16[5,64,1536]{2,1,0:T(8,128)(2,1)}, u32[]{:S(2)}) copy-start(bf16[5,64,1536]{2,1,0:T(8,128)(2,1)} %param.5) | copy-start | bytes 2949124
  7.2 97.9 %all-gather.9.cloned.1.call-start = ((), (), s32[]{:S(2)}) async-start(), calls=%async_computation.4 | async-start | bytes 5308416 | tf_op jit(solution)/shard_map/all_gather | solution.py:56
  7.9 248.8 %all-gather.5.cloned.1.call-start = ((), (), s32[]{:S(2)}) async-start(), calls=%async_computation.2 | async-start | bytes 7962624 | tf_op jit(solution)/shard_map/all_gather | solution.py:83
  8.7 256.2 %all-gather.7.cloned.1.call-start = ((), (), s32[]{:S(2)}) async-start(), calls=%async_computation.3 | async-start | bytes 2654208 | tf_op jit(solution)/shard_map/all_gather | solution.py:90
  52.2 0.9 copy-start.3
  53.2 23.4 %collective-permute-start = (bf16[5,16,1536]{2,1,0:T(8,128)(2,1)S(1)}, bf16[5,16,1536]{2,1,0:T(8,128)(2,1)}, u32[]{:S(2)}, u32[]{:S(2)}) collective-permute-start(bf16[5,16,1536]{2,1,0:T(8,128)(2,1)S(1)} %get-tuple-element.9), channel_id=1, source_target_pairs={{0,1},{1,2},{2,3},{3,4},{4,5},{5,6},{6,7},{8,9},{9,10},{10,11},{11... | collective-permute-start | bytes 737288 | tf_op jit(solution)/shard_map/ppermute | solution.py:18
  56.7 19.8 %collective-permute-start.1 = (bf16[5,16,1536]{2,1,0:T(8,128)(2,1)S(1)}, bf16[5,16,1536]{2,1,0:T(8,128)(2,1)}, u32[]{:S(2)}, u32[]{:S(2)}) collective-permute-start(bf16[5,16,1536]{2,1,0:T(8,128)(2,1)S(1)} %get-tuple-element.10), channel_id=1, source_target_pairs={{1,0},{2,1},{3,2},{4,3},{5,4},{6,5},{7,6},{9,8},{10,9},{11,10},{12... | collective-permute-start | bytes 737288 | tf_op jit(solution)/shard_map/ppermute | solution.py:21
  58.7 394.4 %reduce-scatter.3.cloned.1.call-start = ((), (), s32[]{:S(2)}) async-start(), calls=%async_computation.5 | async-start | bytes 14598144 | tf_op jit(solution)/shard_map/reduce_scatter | solution.py:110
  73.0 3.6 copy-start.4
  256.7 2.7 copy-start.6
  259.4 2.7 copy-start.5
  264.9 4.1 copy-start.7
  268.9 1.4 copy-start.1
  268.9 2.0 copy-start.10
  270.9 3.5 copy-start.9
  274.4 3.6 copy-start.8
  292.7 1.5 copy-start.2
  292.7 271.9 %reduce-scatter.5.cloned.1.call-start = ((), (), s32[]{:S(2)}) async-start(), calls=%async_computation.7 | async-start | bytes 4866048 | tf_op jit(solution)/shard_map/reduce_scatter | solution.py:119
  297.8 290.3 %all-gather.11.cloned.1.call-start = ((), (), s32[]{:S(2)}) async-start(), calls=%async_computation.6 | async-start | bytes 2211840 | tf_op jit(solution)/shard_map/all_gather | solution.py:126
Sparse Core Ops, SparseCore 0:
  10.2 89.9 all-gather.8
  102.4 106.8 all-gather.4
  211.5 51.3 all-gather.6
  292.8 160.1 reduce-scatter.2
  458.4 106.2 reduce-scatter.4
  566.1 21.9 all-gather.10
where the time goes:
time: 602 us; the launch traced here: 600 us
  waiting for transfers between devices  240 us (40%)
  blocking collectives  233 us (39%)
  local copies, waits for them, and re-layouts  47.7 us (8%)
  matrix products  38.4 us (6%)
  other arithmetic  18.6 us (3%)
  between operations  16.1 us (3%)
    reduce_scatter x1, waiting for transfers between devices, shards(): lax.psum_scatter(jnp.stack([column_product(taps_moved[offset_index], prea...  155 us
    psum x1, blocking collectives, shards(): summed = lax.psum(projected, 'teacher')  141 us
    reduce_scatter x1, waiting for transfers between devices, shards(): lax.psum_scatter(column_product(activated_moved, out_grad), ('teacher', '...  70.1 us
    psum x1, blocking collectives, shards(): lax.psum((jnp.sum(inputs_f, axis=0), jnp.sum(inputs_f * inputs_f, axis=0)...  41.2 us
    psum x1, blocking collectives, shards(): squared_total = lax.psum(jnp.sum(misfit * misfit), ('teacher', 'seq'))  40.8 us
    another operation x2, local copies, waits for them, and re-layouts, regroup_columns(): matrix.reshape(count_of_rows, ranks, groups, -1).transpose(0, 2, 1, 3)  14.4 us
    dot_general x4, matrix products, column_product(): lax.dot_general(left, right, (((0,), (0,)), ((), ())), preferred_element_...  14.2 us
    convert_element_type x2, local copies, waits for them, and re-layouts, shards(): activations.reshape(count_of_rows, channel_count).astype(jnp.float32)  13.7 us
  transfers between devices with their start and end apart: 8, of which 3 were waited for; matrix products, arithmetic and copies ran while one was open for 12% of the time, Pallas kernels for 0%

commit v1 on v0

v1 whole, which is shorter than its diff:
```python
import functools

import jax
import jax.numpy as jnp
from jax import lax
from jax.experimental import pallas as pl
from jax.experimental.pallas import tpu as pltpu
from jax.sharding import PartitionSpec as P

TAP_DILATION = 16

slope_const = 0.7978845608
cubic_const = 0.044715

MESH = pl.DeviceIdType.MESH
HBM = pl.BlockSpec(memory_space=pl.ANY)
VMEM = pl.BlockSpec(memory_space=pltpu.VMEM)


class Link:
    def __init__(self, send, recv):
        self.send, self.recv, self.used, self.started = send, recv, 0, []

    def take(self, count):
        first = self.used
        self.used += count
        return first

    def copy(self, src, dst, slot, device):
        return pltpu.make_async_remote_copy(
            src_ref=src,
            dst_ref=dst,
            send_sem=self.send.at[slot],
            recv_sem=self.recv.at[slot],
            device_id=device,
            device_id_type=MESH,
        )

    def start(self, src, dst, slot, device):
        put = self.copy(src, dst, slot, device)
        put.start()
        self.started.append(put)

    def arrived(self, dst, slot, device):
        self.copy(dst, dst, slot, device).wait_recv()

    def drain(self):
        for put in self.started:
            put.wait_send()


class Place:
    def __init__(self, groups, ranks):
        self.groups, self.ranks = groups, ranks
        self.t, self.s = lax.axis_index("teacher"), lax.axis_index("seq")
        self.core = self.t % 2
        self.bit = self.s % 2
        self.col = self.s // 2
        self.cols = ranks // 2
        self.sibling = {"teacher": self.t + 1 - 2 * self.core}
        self.across = {"teacher": (self.t + 2) % groups}
        self.partner = {"seq": self.s + 1 - 2 * self.bit}

    def later(self, step):
        return (self.s + step) % self.ranks

    def earlier(self, step):
        return (self.s + self.ranks - step) % self.ranks

    def barrier(self, seq=True, teacher=True):
        sem = pltpu.get_barrier_semaphore()
        count = 0
        if seq:
            for step in range(1, self.ranks):
                pl.semaphore_signal(
                    sem, inc=1, device_id={"seq": self.later(step)}, device_id_type=MESH
                )
                count += 1
        if teacher:
            for step in range(1, self.groups):
                pl.semaphore_signal(
                    sem,
                    inc=1,
                    device_id={"teacher": (self.t + step) % self.groups},
                    device_id_type=MESH,
                )
                count += 1
        pl.semaphore_wait(sem, count)


class Gather:
    def __init__(self, place, link, source, piece, sibling_piece=None):
        self.place, self.link, self.source = place, link, source
        self.piece, self.sibling_piece = piece, sibling_piece
        self.down = link.take(place.cols)
        self.over = link.take(place.cols)
        self.side = link.take(place.ranks) if sibling_piece else None

    def shard(self, step, bit):
        place = self.place
        return ((place.col + place.cols - step) % place.cols) * 2 + bit

    def start(self):
        place, link = self.place, self.link
        for step in range(1, place.cols):
            peer = ((place.col + step) % place.cols) * 2 + place.bit
            link.start(self.source, self.piece(place.s), self.down + step, {"seq": peer})
        link.start(self.source, self.piece(place.s), self.over, place.partner)

    def forward(self):
        place, link = self.place, self.link
        for step in range(1, place.cols):
            ref = self.piece(self.shard(step, place.bit))
            link.arrived(ref, self.down + step, place.partner)
            link.start(ref, ref, self.over + step, place.partner)
            if self.side is not None:
                link.start(ref, ref, self.side + step, place.sibling)

    def collect(self):
        place, link = self.place, self.link
        for step in range(place.cols):
            ref = self.piece(self.shard(step, 1 - place.bit))
            link.arrived(ref, self.over + step, place.partner)
            if self.side is not None:
                link.start(ref, ref, self.side + place.cols + step, place.sibling)

    def finish(self):
        place, link = self.place, self.link
        if self.side is None:
            return
        for step in range(1, place.cols):
            ref = self.sibling_piece(self.shard(step, place.bit))
            link.arrived(ref, self.side + step, place.sibling)
        for step in range(place.cols):
            ref = self.sibling_piece(self.shard(step, 1 - place.bit))
            link.arrived(ref, self.side + place.cols + step, place.sibling)


def total_of(place, link, own, stage_t, stage_s):
    to_t, to_s = link.take(place.groups), link.take(place.ranks)

    def first():
        stage_t[place.t] = own[...]
        for step in range(1, place.groups):
            link.start(
                own,
                stage_t.at[place.t],
                to_t + step,
                {"teacher": (place.t + step) % place.groups},
            )

    def second():
        for step in range(1, place.groups):
            giver = (place.t + place.groups - step) % place.groups
            link.arrived(stage_t.at[giver], to_t + step, place.sibling)
        summed = stage_t[0]
        for group in range(1, place.groups):
            summed = summed + stage_t[group]
        stage_s[place.s] = summed
        for step in range(1, place.ranks):
            link.start(
                stage_s.at[place.s],
                stage_s.at[place.s],
                to_s + step,
                {"seq": place.later(step)},
            )

    def third():
        for step in range(1, place.ranks):
            link.arrived(stage_s.at[place.earlier(step)], to_s + step, place.partner)
        summed = stage_s[0]
        for rank in range(1, place.ranks):
            summed = summed + stage_s[rank]
        return summed

    return first, second, third


def projection_kernel(groups, ranks, proj, stats, full, totals, stage_t, stage_s, send, recv, local):
    place, link = Place(groups, ranks), Link(send, recv)
    place.barrier()
    keep = pltpu.make_async_copy(proj, full.at[place.s], local.at[0])
    keep.start()
    first, second, third = total_of(place, link, stats, stage_t, stage_s)
    gather = Gather(place, link, proj, lambda j: full.at[j])
    first()
    gather.start()
    second()
    totals[...] = third()
    gather.forward()
    gather.collect()
    keep.wait()
    link.drain()


def forward_kernel(
    groups, ranks, terms, dilated, pointwise, panels, hidden,
    terms_all, dilated_all, pointwise_all, panels_all, halo, send, recv, local,
):
    place, link = Place(groups, ranks), Link(send, recv)
    half_d, half_p = dilated.shape[2] // 2, pointwise.shape[1] // 2
    bins = hidden.shape[1]
    place.barrier()

    def columns(core, half):
        return pl.ds(pl.multiple_of(core * half, half), half)

    mine_d, mine_p = columns(place.core, half_d), columns(place.core, half_p)
    other_d, other_p = columns(1 - place.core, half_d), columns(1 - place.core, half_p)
    to_t, to_s, edges = link.take(groups), link.take(ranks), link.take(2)
    after, before = {"seq": place.later(1)}, {"seq": place.earlier(1)}
    link.start(hidden.at[:, pl.ds(bins - TAP_DILATION, TAP_DILATION)], halo.at[0], edges, after)
    link.start(hidden.at[:, pl.ds(0, TAP_DILATION)], halo.at[1], edges + 1, before)
    for step in range(1, groups):
        taker = (place.t + step) % groups
        link.start(terms.at[taker], terms_all.at[place.t], to_t + step, {"teacher": taker})
    gather_d = Gather(
        place,
        link,
        dilated.at[:, :, mine_d],
        lambda j: dilated_all.at[:, j, :, mine_d],
        lambda j: dilated_all.at[:, j, :, other_d],
    )
    gather_p = Gather(
        place,
        link,
        pointwise.at[:, mine_p],
        lambda j: pointwise_all.at[j, :, mine_p],
        lambda j: pointwise_all.at[j, :, other_p],
    )
    gather_d.start()
    gather_p.start()
    for step in range(1, ranks):
        taker = place.later(step)
        link.start(panels.at[taker], panels_all.at[place.s], to_s + step, {"seq": taker})
    keeps = [
        pltpu.make_async_copy(terms.at[place.t], terms_all.at[place.t], local.at[0]),
        pltpu.make_async_copy(dilated, dilated_all.at[:, place.s], local.at[1]),
        pltpu.make_async_copy(pointwise, pointwise_all.at[place.s], local.at[2]),
        pltpu.make_async_copy(panels.at[place.s], panels_all.at[place.s], local.at[3]),
    ]
    for keep in keeps:
        keep.start()
    gather_d.forward()
    gather_p.forward()
    gather_d.collect()
    gather_p.collect()
    gather_d.finish()
    gather_p.finish()
    link.arrived(halo.at[0], edges, after)
    link.arrived(halo.at[1], edges + 1, before)
    for step in range(1, groups):
        giver = (place.t + groups - step) % groups
        link.arrived(terms_all.at[giver], to_t + step, place.sibling)
    for step in range(1, ranks):
        link.arrived(panels_all.at[place.earlier(step)], to_s + step, place.partner)
    for keep in keeps:
        keep.wait()
    link.drain()


def backward_kernel(
    groups, ranks, slopes, partial, loss,
    slopes_all, shares, loss_total,
    from_core, from_chip, pieces, stage_t, stage_s, send, recv, local,
):
    place, link = Place(groups, ranks), Link(send, recv)
    width = partial.shape[1] // groups
    rows = partial.shape[0] // ranks
    place.barrier()
    keep = pltpu.make_async_copy(slopes, slopes_all.at[place.s], local.at[0])
    keep.start()
    to_core, to_chip, to_s, to_t = (link.take(count) for count in (1, 1, ranks, groups))
    high = place.t // 2

    def columns(index, size):
        return pl.ds(pl.multiple_of(index * size, size), size)

    link.start(partial.at[:, columns(1 - place.core, 2 * width)], from_core, to_core, place.sibling)
    first, second, third = total_of(place, link, loss, stage_t, stage_s)
    first()
    gather = Gather(place, link, slopes, lambda j: slopes_all.at[j])
    gather.start()
    link.arrived(from_core, to_core, place.sibling)
    mine = columns(place.core, 2 * width)

    @pl.loop(0, ranks)
    def _(rank):
        span = pl.ds(pl.multiple_of(rank * rows, rows), rows)
        from_core[span] = from_core[span] + partial[span, mine]

    link.start(from_core.at[:, columns(1 - high, width)], from_chip, to_chip, place.across)
    second()
    loss_total[...] = third()
    link.arrived(from_chip, to_chip, place.across)
    kept = columns(high, width)

    @pl.loop(0, ranks)
    def _(rank):
        span = pl.ds(pl.multiple_of(rank * rows, rows), rows)
        from_chip[span] = from_chip[span] + from_core[span, kept]

    for step in range(1, ranks):
        taker = place.later(step)
        span = pl.ds(pl.multiple_of(taker * rows, rows), rows)
        link.start(from_chip.at[span], pieces.at[place.s], to_s + step, {"seq": taker})
    gather.forward()
    own = pl.ds(pl.multiple_of(place.s * rows, rows), rows)
    pieces[place.s] = from_chip[own]
    for step in range(1, ranks):
        link.arrived(pieces.at[place.earlier(step)], to_s + step, place.partner)
    summed = pieces[0]
    for rank in range(1, ranks):
        summed = summed + pieces[rank]
    slot = place.core * 2 + high
    shares[slot] = summed
    for step in range(1, groups):
        link.start(
            shares.at[slot],
            shares.at[slot],
            to_t + step,
            {"teacher": (place.t + step) % groups},
        )
    gather.collect()
    for step in range(1, groups):
        giver = (place.t + groups - step) % groups
        link.arrived(shares.at[(giver % 2) * 2 + giver // 2], to_t + step, place.sibling)
    keep.wait()
    link.drain()


def share_kernel(groups, ranks, partial, out, from_core, from_chip, send, recv):
    place, link = Place(groups, ranks), Link(send, recv)
    taps, rows, width = partial.shape
    half = width // 2
    place.barrier(seq=False)
    a, b, c = link.take(taps), link.take(taps), link.take(taps)

    def columns(core):
        return pl.ds(pl.multiple_of(core * half, half), half)

    mine, other = columns(place.core), columns(1 - place.core)
    for tap in range(taps):
        link.start(partial.at[tap, :, other], from_core.at[tap], a + tap, place.sibling)
    for tap in range(taps):
        link.arrived(from_core.at[tap], a + tap, place.sibling)
        from_core[tap] = from_core[tap] + partial[tap, :, mine]
        link.start(from_core.at[tap], from_chip.at[tap], b + tap, place.across)
    for tap in range(taps):
        link.arrived(from_chip.at[tap], b + tap, place.across)
        out[tap, :, mine] = from_chip[tap] + from_core[tap]
        link.start(out.at[tap, :, mine], out.at[tap, :, mine], c + tap, place.sibling)
    for tap in range(taps):
        link.arrived(out.at[tap, :, other], c + tap, place.sibling)
    link.drain()


def exchange(kernel, number, groups, ranks, args, specs, outs, out_specs, scratch, copies, locals_):
    sems = [pltpu.SemaphoreType.DMA((copies,)), pltpu.SemaphoreType.DMA((copies,))]
    if locals_:
        sems.append(pltpu.SemaphoreType.DMA((locals_,)))
    return pl.pallas_call(
        functools.partial(kernel, groups, ranks),
        out_shape=[jax.ShapeDtypeStruct(shape, kind) for shape, kind in outs],
        in_specs=specs,
        out_specs=out_specs,
        scratch_shapes=[pltpu.VMEM(shape, kind) for shape, kind in scratch] + sems,
        compiler_params=pltpu.CompilerParams(
            collective_id=number, has_side_effects=True, vmem_limit_bytes=40 * 1024 * 1024
        ),
    )(*args)


def gelu_tanh(value):
    inside = slope_const * (value + cubic_const * value * value * value)
    return 0.5 * value * (1.0 + jnp.tanh(inside))


def gelu_slope(value):
    inside = slope_const * (value + cubic_const * value * value * value)
    tangent = jnp.tanh(inside)
    return 0.5 * (1.0 + tangent) + 0.5 * value * (1.0 - tangent * tangent) * slope_const * (
        1.0 + 3.0 * cubic_const * value * value
    )


def column_product(left, right):
    return lax.dot_general(
        left, right, (((0,), (0,)), ((), ())), preferred_element_type=jnp.float32
    )


def shards(activations, teacher_maps, projection, dilated_weight, pointwise_weight):
    groups = lax.axis_size("teacher")
    ranks = lax.axis_size("seq")
    f32, bf16 = jnp.float32, jnp.bfloat16
    win_grp, bins, channels = activations.shape
    branch = dilated_weight.shape[2]
    panel = dilated_weight.shape[0]
    features = projection.shape[1]
    rows = win_grp * bins
    total_rows = rows * groups * ranks
    rank = lax.axis_index("seq")

    inputs_f = activations.reshape(rows, channels).astype(f32)
    stats = jnp.concatenate(
        [
            jnp.sum(inputs_f, axis=0, keepdims=True),
            jnp.sum(inputs_f * inputs_f, axis=0, keepdims=True),
            jnp.zeros((6, channels), f32),
        ]
    )
    proj_full, totals = exchange(
        projection_kernel, 0, groups, ranks,
        (projection[0], stats), [HBM, VMEM],
        [((ranks, features, channels), bf16), ((8, channels), f32)], [HBM, VMEM],
        [((groups, 8, channels), f32), ((ranks, 8, channels), f32)],
        2 * ranks + groups, 1,
    )
    channel_mean = totals[0] / total_rows
    channel_var = totals[1] / total_rows - channel_mean * channel_mean
    normed = (inputs_f - channel_mean) * lax.rsqrt(channel_var + 1e-05)
    hidden = gelu_tanh(normed).astype(bf16)
    hidden_3d = hidden.reshape(win_grp, bins, channels)
    panels = jnp.stack([hidden[:, j * panel : (j + 1) * panel] for j in range(ranks)])
    terms = jnp.dot(
        teacher_maps[0].reshape(groups * rows, -1),
        proj_full.reshape(ranks * features, channels),
        preferred_element_type=f32,
    ).astype(bf16)

    terms_all, dilated_all, pointwise_all, panels_all, halo = exchange(
        forward_kernel, 1, groups, ranks,
        (
            terms.reshape(groups, rows, channels),
            dilated_weight.transpose(1, 0, 2),
            pointwise_weight,
            panels,
            hidden_3d,
        ),
        [HBM] * 5,
        [
            ((groups, rows, channels), bf16),
            ((3, ranks, panel, branch), bf16),
            ((ranks,) + pointwise_weight.shape, bf16),
            ((ranks, rows, panel), bf16),
            ((2, win_grp, TAP_DILATION, channels), bf16),
        ],
        [HBM] * 5,
        [],
        5 * ranks + groups + 2, 4,
    )
    target = terms_all[0].astype(f32)
    for group in range(1, groups):
        target = target + terms_all[group].astype(f32)
    target = target / groups

    low = jnp.where(rank > 0, halo[0], jnp.zeros_like(halo[0]))
    high = jnp.where(rank < ranks - 1, halo[1], jnp.zeros_like(halo[1]))
    padded = jnp.concatenate([low, hidden_3d, high], axis=1)
    preact = jnp.zeros((rows, branch), f32)
    for tap in range(3):
        shifted = padded[:, tap * TAP_DILATION : tap * TAP_DILATION + bins].reshape(rows, channels)
        preact = preact + jnp.dot(
            shifted, dilated_all[tap].reshape(channels, branch), preferred_element_type=f32
        )
    activated = gelu_tanh(preact).astype(bf16)
    pointwise_full = pointwise_all.reshape(branch, channels)
    student = inputs_f + jnp.dot(activated, pointwise_full, preferred_element_type=f32)
    misfit = student - target
    squared = jnp.sum(misfit * misfit)
    out_grad = (misfit / channels).astype(bf16)
    back_grad = lax.dot_general(
        out_grad, pointwise_full, (((1,), (1,)), ((), ())), preferred_element_type=f32
    )
    preact_grad = (back_grad * gelu_slope(preact)).astype(bf16)
    pointwise_part = column_product(activated, out_grad)

    slopes_all, shares, loss_total = exchange(
        backward_kernel, 2, groups, ranks,
        (preact_grad, pointwise_part, jnp.full((8, 128), squared, f32)),
        [HBM, VMEM, VMEM],
        [
            ((ranks, rows, branch), bf16),
            ((groups, branch // ranks, channels // groups), f32),
            ((8, 128), f32),
        ],
        [HBM, VMEM, VMEM],
        [
            ((branch, channels // 2), f32),
            ((branch, channels // groups), f32),
            ((ranks, branch // ranks, channels // groups), f32),
            ((groups, 8, 128), f32),
            ((ranks, 8, 128), f32),
        ],
        3 * ranks + 2 * groups + 2, 1,
    )
    loss_mean = 0.5 * loss_total[0, 0] / (channels * total_rows)
    pointwise_grad = shares.transpose(1, 0, 2).reshape(branch // ranks, channels)

    def windows(blocks):
        return (
            blocks.reshape(ranks, win_grp, bins, -1)
            .transpose(1, 0, 2, 3)
            .reshape(win_grp, ranks * bins, -1)
        )

    hidden_w = jnp.pad(windows(panels_all), ((0, 0), (TAP_DILATION, TAP_DILATION), (0, 0)))
    slopes_w = windows(slopes_all).reshape(win_grp * ranks * bins, branch)
    partial = jnp.stack(
        [
            column_product(
                hidden_w[:, tap * TAP_DILATION : tap * TAP_DILATION + ranks * bins].reshape(
                    win_grp * ranks * bins, panel
                ),
                slopes_w,
            )
            for tap in range(3)
        ]
    )
    (dilated_grad,) = exchange(
        share_kernel, 3, groups, ranks,
        (partial,), [VMEM],
        [((3, panel, branch), f32)], [VMEM],
        [((3, panel, branch // 2), f32), ((3, panel, branch // 2), f32)],
        9, 0,
    )
    return (loss_mean, dilated_grad.transpose(1, 0, 2), pointwise_grad)


def solution(mesh):
    in_specs = (
        P("teacher", "seq", None),
        P("teacher", None, "seq", None),
        P("teacher", "seq", None),
        P("seq", None, None),
        P("seq", None),
    )
    out_specs = (P(), P("seq", None, None), P("seq", None))
    return jax.shard_map(shards, mesh=mesh, in_specs=in_specs, out_specs=out_specs, check_vma=False)
```

time: 602 us -> 366 us (0.61)
  Pallas kernels: 0 us -> 317 us
  waiting for transfers between devices: 240 us -> 0 us
  blocking collectives: 233 us -> 0 us
  local copies, waits for them, and re-layouts: 47.7 us -> 19.2 us
  matrix products: 38.4 us -> 20.6 us
  other arithmetic: 18.6 us -> 3.62 us
  between operations: 16.1 us -> 2.71 us
    pallas_call x0 -> x4, Pallas kernels: none -> 317 us  [exchange(): pl.pallas_call(functools.partial(kernel, groups, ranks), out_shape=[jax.S...]
    reduce_scatter x2 -> x0, waiting for transfers between devices: 225 us -> none  [the longest x1 155 us: shards(): lax.psum_scatter(jnp.stack([column_product(taps_moved[offset_index], prea...]
    psum x3 -> x0, blocking collectives: 223 us -> none  [the longest x1 141 us: shards(): summed = lax.psum(projected, 'teacher')]
    another operation x2 -> x1, local copies, waits for them, and re-layouts: 14.4 us -> 0.11 us  [shards(): jnp.stack([hidden[:, j * panel:(j + 1) * panel] for j in range(ranks)])]
    convert_element_type x3 -> x0, local copies, waits for them, and re-layouts: 14 us -> none  [the longest x2 13.7 us: shards(): activations.reshape(count_of_rows, channel_count).astype(jnp.float32)]
    all_gather x4 -> x0, waiting for transfers between devices: 13.7 us -> none  [the longest x1 13.7 us: shards(): lax.all_gather(dilated_share, 'teacher', axis=0, tiled=True)]
    transpose x4 -> x0, local copies, waits for them, and re-layouts: 12.8 us -> none  [regroup_columns(): return matrix.reshape(count_of_rows, ranks, groups, -1).transpose(0, 2, 1...]
    another operation x1, other arithmetic: 11.1 us -> 0.12 us  [shards(): jnp.stack([column_product(hidden_w[:, tap * TAP_DILATION:tap * TAP_DILATI...]
  transfers between devices with their start and end apart: 8 -> 0, of which waited for: 3 -> 0; matrix products, arithmetic and copies ran while one was open for 12% -> 0% of each run, Pallas kernels for 0% -> 0%
where the time goes in v1:
time: 366 us; the launch traced here: 363 us
  Pallas kernels  317 us (87%)
  matrix products  20.6 us (6%)
  local copies, waits for them, and re-layouts  19.2 us (5%)
    pallas_call x4, Pallas kernels, exchange(): pl.pallas_call(functools.partial(kernel, groups, ranks), out_shape=[jax.S...  317 us
    unnamed x32, local copies, waits for them, and re-layouts  9.47 us
    dot_general x1, matrix products, shards(): jnp.dot(teacher_maps[0].reshape(groups * rows, -1), proj_full.reshape(ran...  7.96 us

profile of v1, /device:TPU:11, one launch (start us, length us, event | category | flops | bytes accessed | tf_op | source)
XLA Modules:
  0.0 363.0 jit_solution(17203505209887559142)
XLA Ops:
  0.6 1.6 convert_reduce_fusion
  2.4 1.1 copy-done.1
  3.5 100.5 %shard_map.76 = (bf16[8,192,1536]{2,1,0:T(8,128)(2,1)S(1)}, f32[8,1536]{1,0:T(8,128)S(1)}) custom-call(bf16[192,1536]{1,0:T(8,128)(2,1)S(1)} %bitcast.117, f32[8,1536]{1,0:T(8,128)S(1)} %maximum_maximum_fusion.stats), custom_call_target="tpu_custom_call" | custom-call | tf_op jit(solution)/shard_map/pallas_call | solution.py:362
  104.0 0.8 fusion.7
  105.4 0.8 fusion.12.hidden
  106.2 0.9 copy-done.11
  107.1 8.0 %convolution_convert_fusion = bf16[1536,1280]{0,1:T(8,128)(2,1)} fusion(bf16[1280,1536]{1,0:T(8,128)(2,1)S(1)} %bitcast.135, bf16[1536,1536]{1,0:T(8,128)(2,1)S(1)} %bitcast.119), kind=kOutput, calls=%fused_computation | convolution fusion | flops 6041763840 | bytes 12582912 | tf_op jit(solution)/shard_map/dot_general | solution.py:426
  115.1 92.1 %shard_map.77 = (bf16[4,320,1536]{2,1,0:T(8,128)(2,1)S(1)}, bf16[3,8,192,768]{3,2,1,0:T(8,128)(2,1)}, bf16[8,96,1536]{2,1,0:T(8,128)(2,1)S(1)}, bf16[8,320,192]{...) custom-call(bf16[4,320,1536]{2,1,0:T(8,128)(2,1)} %bitcast.124, bf16[3,192,768]{2,1,0:T(8,128)(2,1)S(1)} %bitcast.116, ...), custom_call_target="tpu_custom_call" | custom-call | tf_op jit(solution)/shard_map/pallas_call | solution.py:362
  207.2 2.0 copy-done.3
  209.2 6.9 %fusion.44 = (bf16[1,8,192,768]{3,2,1,0:T(8,128)(2,1)}, bf16[1,8,192,768]{3,2,1,0:T(8,128)(2,1)}, bf16[1,8,192,768]{3,2,1,0:T(8,128)(2,1)}) fusion(bf16[3,8,192,768]{3,2,1,0:T(8,128)(2,1)} %get-tuple-element.16), kind=kLoop, calls=%fused_computation.76 | loop fusion | bytes 14155776 | tf_op jit(solution)/shard_map/slice | solution.py:465
  216.4 1.5 copy-done.10
  217.8 0.9 fusion.45
  219.5 0.9 convolution_add_fusion.2
  221.2 0.9 convolution_add_fusion.1
  223.1 4.1 %multiply_reduce_fusion = (f32[]{:T(128)}, f32[320,1536]{1,0:T(8,128)S(1)}) fusion(bf16[4,320,1536]{2,1,0:T(8,128)(2,1)} %copy-done.3, bf16[768,1536]{1,0:T(8,128)(2,1)S(1)} %bitcast.120, f32[320,768]{1,0:T(8,128)S(1)} %convolution_add_fusion.1, bf16[320,1536]{1,0:T(8,128)(2,1)S(1)} %bitcast.122), kind=kOutput, calls=%fused_computation.26 | convolution fusion | flops 763576320 | bytes 10223620 | tf_op jit(solution)/shard_map/dot_general | solution.py:469
  227.2 1.6 fusion.30.partial
  228.8 1.3 fusion.19.slopes
  230.7 98.1 %shard_map.78 = (bf16[8,320,768]{2,1,0:T(8,128)(2,1)S(1)}, f32[4,96,384]{2,1,0:T(8,128)S(1)}, f32[8,128]{1,0:T(8,128)S(1)}) custom-call(bf16[320,768]{1,0:T(8,128)(2,1)S(1)} %fusion.19.slopes, f32[768,1536]{1,0:T(8,128)S(1)} %fusion.30.partial, f32[8,128]{1,0:T(8,128)S(1)} %broadcast_in_dim.17.loss), custom_call_target="tpu_custom_call" | custom-call | tf_op jit(solution)/shard_map/pallas_call | solution.py:362
  329.4 1.0 convolution_bitcast_fusion.1
  330.4 1.0 fusion.20
  331.4 1.0 convolution_bitcast_fusion
  332.5 26.1 %shard_map.79 = f32[3,192,768]{2,1,0:T(8,128)S(1)} custom-call(f32[3,192,768]{2,1,0:T(8,128)S(1)} %pad_maximum_fusion.partial), custom_call_target="tpu_custom_call" | custom-call | tf_op jit(solution)/shard_map/pallas_call | solution.py:362
  358.6 0.9 copy.14
  360.7 1.2 copy.31
  (42 shorter events, 5.3 us)
Async XLA Ops:
  0.6 103.4 %copy-start.6 = (bf16[5,64,1536]{2,1,0:T(8,128)(2,1)S(1)}, bf16[5,64,1536]{2,1,0:T(8,128)(2,1)}, u32[]{:S(2)}) copy-start(bf16[5,64,1536]{2,1,0:T(8,128)(2,1)} %param.5) | copy-start | bytes 2949124
  2.4 1.1 copy-start.1
  105.0 2.1 copy-start.11
  107.1 8.0 %copy-start = (bf16[192,3,768]{2,0,1:T(8,128)(2,1)S(1)}, bf16[192,3,768]{2,0,1:T(8,128)(2,1)}, u32[]{:S(2)}) copy-start(bf16[192,3,768]{2,0,1:T(8,128)(2,1)} %param.8) | copy-start | bytes 2654212
  107.1 8.0 %copy-start.2 = (bf16[96,1536]{1,0:T(8,128)(2,1)S(1)}, bf16[96,1536]{1,0:T(8,128)(2,1)}, u32[]{:S(2)}) copy-start(bf16[96,1536]{1,0:T(8,128)(2,1)} %pointwise.1) | copy-start | bytes 884740
  207.2 2.0 copy-start.3
  209.2 6.9 %copy-start.4 = (bf16[8,96,1536]{2,1,0:T(8,128)(2,1)}, bf16[8,96,1536]{2,1,0:T(8,128)(2,1)S(1)}, u32[]{:S(2)}) copy-start(bf16[8,96,1536]{2,1,0:T(8,128)(2,1)S(1)} %get-tuple-element.17) | copy-start | bytes 7077892
  216.2 1.7 copy-start.10
  217.8 1.7 copy-start.9
  219.5 1.7 copy-start.8
  221.2 1.7 copy-start.5
  221.2 1.9 copy-start.7

commit v2 on v1

--- a/solution.py
+++ b/solution.py
@@ -89,51 +89,43 @@
 
 
 class Gather:
-    def __init__(self, place, link, source, piece, sibling_piece=None):
-        self.place, self.link, self.source = place, link, source
-        self.piece, self.sibling_piece = piece, sibling_piece
-        self.down = link.take(place.cols)
-        self.over = link.take(place.cols)
-        self.side = link.take(place.ranks) if sibling_piece else None
-
-    def shard(self, step, bit):
+    def __init__(self, place, link, source, piece, chunks, spread=None):
+        self.place, self.link, self.source, self.piece = place, link, source, piece
+        self.chunks, self.spread = chunks, spread
+        self.down = [link.take(place.cols) for _ in range(chunks)]
+        self.over = [link.take(place.cols) for _ in range(chunks)]
+
+    def shard(self, index):
         place = self.place
-        return ((place.col + place.cols - step) % place.cols) * 2 + bit
+        bit = place.bit if index < place.cols else 1 - place.bit
+        return ((place.col + place.cols - index % place.cols) % place.cols) * 2 + bit
 
     def start(self):
         place, link = self.place, self.link
-        for step in range(1, place.cols):
-            peer = ((place.col + step) % place.cols) * 2 + place.bit
-            link.start(self.source, self.piece(place.s), self.down + step, {"seq": peer})
-        link.start(self.source, self.piece(place.s), self.over, place.partner)
-
-    def forward(self):
+        for chunk in range(self.chunks):
+            source, target = self.source(chunk), self.piece(place.s, chunk)
+            link.start(source, target, self.over[chunk], place.partner)
+            for step in range(1, place.cols):
+                peer = ((place.col + step) % place.cols) * 2 + place.bit
+                link.start(source, target, self.down[chunk] + step, {"seq": peer})
+
+    def forward(self, chunk):
         place, link = self.place, self.link
         for step in range(1, place.cols):
-            ref = self.piece(self.shard(step, place.bit))
-            link.arrived(ref, self.down + step, place.partner)
-            link.start(ref, ref, self.over + step, place.partner)
-            if self.side is not None:
-                link.start(ref, ref, self.side + step, place.sibling)
-
-    def collect(self):
+            shard = self.shard(step)
+            ref = self.piece(shard, chunk)
+            link.arrived(ref, self.down[chunk] + step, place.partner)
+            link.start(ref, ref, self.over[chunk] + step, place.partner)
+            if self.spread is not None:
+                self.spread(shard, chunk, step)
+
+    def collect(self, chunk):
         place, link = self.place, self.link
         for step in range(place.cols):
-            ref = self.piece(self.shard(step, 1 - place.bit))
-            link.arrived(ref, self.over + step, place.partner)
-            if self.side is not None:
-                link.start(ref, ref, self.side + place.cols + step, place.sibling)
-
-    def finish(self):
-        place, link = self.place, self.link
-        if self.side is None:
-            return
-        for step in range(1, place.cols):
-            ref = self.sibling_piece(self.shard(step, place.bit))
-            link.arrived(ref, self.side + step, place.sibling)
-        for step in range(place.cols):
-            ref = self.sibling_piece(self.shard(step, 1 - place.bit))
-            link.arrived(ref, self.side + place.cols + step, place.sibling)
+            shard = self.shard(place.cols + step)
+            link.arrived(self.piece(shard, chunk), self.over[chunk] + step, place.partner)
+            if self.spread is not None:
+                self.spread(shard, chunk, place.cols + step)
 
 
 def total_of(place, link, own, stage_t, stage_s):
@@ -176,77 +168,127 @@
     return first, second, third
 
 
-def projection_kernel(groups, ranks, proj, stats, full, totals, stage_t, stage_s, send, recv, local):
+def columns(index, size):
+    return pl.ds(pl.multiple_of(index * size, size), size)
+
+
+def projection_kernel(
+    groups, ranks, proj, dilated, stats, full, dilated_all, totals,
+    stage_t, stage_s, send, recv, local,
+):
     place, link = Place(groups, ranks), Link(send, recv)
+    chunks = 4
+    width = proj.shape[1] // chunks
+    half = dilated.shape[2] // 2
+    high = place.t // 2
+    mine, other = columns(place.core, half), columns(1 - place.core, half)
+    taps = (2 * high, 1, 2 - 2 * high)
+    side, across = [link.take(ranks) for _ in taps], link.take(ranks)
+
+    def to_sibling(shard, chunk, index):
+        ref = dilated_all.at[taps[chunk], shard, :, mine]
+        link.start(ref, ref, side[chunk] + index, place.sibling)
+
+    def spread(shard, chunk, index):
+        if chunk == 0:
+            ref = dilated_all.at[taps[0], shard, :, mine]
+            link.start(ref, ref, across + index, place.across)
+        to_sibling(shard, chunk, index)
+
     place.barrier()
-    keep = pltpu.make_async_copy(proj, full.at[place.s], local.at[0])
-    keep.start()
+    keeps = [
+        pltpu.make_async_copy(proj, full.at[place.s], local.at[0]),
+        pltpu.make_async_copy(dilated, dilated_all.at[:, place.s], local.at[1]),
+    ]
+    for keep in keeps:
+        keep.start()
     first, second, third = total_of(place, link, stats, stage_t, stage_s)
-    gather = Gather(place, link, proj, lambda j: full.at[j])
+    gather = Gather(
+        place,
+        link,
+        lambda q: proj.at[:, pl.ds(q * width, width)],
+        lambda j, q: full.at[j, :, pl.ds(q * width, width)],
+        chunks,
+    )
+    gather_d = Gather(
+        place,
+        link,
+        lambda q: dilated.at[taps[q], :, mine],
+        lambda j, q: dilated_all.at[taps[q], j, :, mine],
+        2,
+        spread,
+    )
     first()
+    gather_d.start()
     gather.start()
     second()
+    for chunk in range(2):
+        gather_d.forward(chunk)
+        gather.forward(chunk)
+    for chunk in range(2):
+        gather_d.collect(chunk)
+        gather.forward(2 + chunk)
+    for index in range(1, ranks):
+        shard = gather_d.shard(index)
+        link.arrived(dilated_all.at[taps[2], shard, :, mine], across + index, place.across)
+        to_sibling(shard, 2, index)
     totals[...] = third()
-    gather.forward()
-    gather.collect()
-    keep.wait()
+    for chunk in range(chunks):
+        gather.collect(chunk)
+    for index in range(1, ranks):
+        for chunk in range(3):
+            ref = dilated_all.at[taps[chunk], gather_d.shard(index), :, other]
+            link.arrived(ref, side[chunk] + index, place.sibling)
+    for keep in keeps:
+        keep.wait()
     link.drain()
 
 
 def forward_kernel(
-    groups, ranks, terms, dilated, pointwise, panels, hidden,
-    terms_all, dilated_all, pointwise_all, panels_all, halo, send, recv, local,
+    groups, ranks, terms, pointwise, panels, hidden,
+    terms_all, pointwise_all, panels_all, halo, send, recv, local,
 ):
     place, link = Place(groups, ranks), Link(send, recv)
-    half_d, half_p = dilated.shape[2] // 2, pointwise.shape[1] // 2
+    half = pointwise.shape[1] // 2
     bins = hidden.shape[1]
     place.barrier()
-
-    def columns(core, half):
-        return pl.ds(pl.multiple_of(core * half, half), half)
-
-    mine_d, mine_p = columns(place.core, half_d), columns(place.core, half_p)
-    other_d, other_p = columns(1 - place.core, half_d), columns(1 - place.core, half_p)
-    to_t, to_s, edges = link.take(groups), link.take(ranks), link.take(2)
+    mine, other = columns(place.core, half), columns(1 - place.core, half)
+    to_t, to_s, edges, side = (link.take(count) for count in (groups, ranks, 2, ranks))
     after, before = {"seq": place.later(1)}, {"seq": place.earlier(1)}
-    link.start(hidden.at[:, pl.ds(bins - TAP_DILATION, TAP_DILATION)], halo.at[0], edges, after)
-    link.start(hidden.at[:, pl.ds(0, TAP_DILATION)], halo.at[1], edges + 1, before)
+
+    def spread(shard, chunk, index):
+        ref = pointwise_all.at[shard, :, mine]
+        link.start(ref, ref, side + index, place.sibling)
+
     for step in range(1, groups):
         taker = (place.t + step) % groups
         link.start(terms.at[taker], terms_all.at[place.t], to_t + step, {"teacher": taker})
-    gather_d = Gather(
+    gather = Gather(
         place,
         link,
-        dilated.at[:, :, mine_d],
-        lambda j: dilated_all.at[:, j, :, mine_d],
-        lambda j: dilated_all.at[:, j, :, other_d],
-    )
-    gather_p = Gather(
-        place,
-        link,
-        pointwise.at[:, mine_p],
-        lambda j: pointwise_all.at[j, :, mine_p],
-        lambda j: pointwise_all.at[j, :, other_p],
-    )
-    gather_d.start()
-    gather_p.start()
+        lambda q: pointwise.at[:, mine],
+        lambda j, q: pointwise_all.at[j, :, mine],
+        1,
+        spread,
+    )
+    gather.start()
+    link.start(hidden.at[:, pl.ds(bins - TAP_DILATION, TAP_DILATION)], halo.at[0], edges, after)
+    link.start(hidden.at[:, pl.ds(0, TAP_DILATION)], halo.at[1], edges + 1, before)
     for step in range(1, ranks):
         taker = place.later(step)
         link.start(panels.at[taker], panels_all.at[place.s], to_s + step, {"seq": taker})
     keeps = [
         pltpu.make_async_copy(terms.at[place.t], terms_all.at[place.t], local.at[0]),
-        pltpu.make_async_copy(dilated, dilated_all.at[:, place.s], local.at[1]),
-        pltpu.make_async_copy(pointwise, pointwise_all.at[place.s], local.at[2]),
-        pltpu.make_async_copy(panels.at[place.s], panels_all.at[place.s], local.at[3]),
+        pltpu.make_async_copy(pointwise, pointwise_all.at[place.s], local.at[1]),
+        pltpu.make_async_copy(panels.at[place.s], panels_all.at[place.s], local.at[2]),
     ]
     for keep in keeps:
         keep.start()
-    gather_d.forward()
-    gather_p.forward()
-    gather_d.collect()
-    gather_p.collect()
-    gather_d.finish()
-    gather_p.finish()
+    gather.forward(0)
+    gather.collect(0)
+    for index in range(1, ranks):
+        ref = pointwise_all.at[gather.shard(index), :, other]
+        link.arrived(ref, side + index, place.sibling)
     link.arrived(halo.at[0], edges, after)
     link.arrived(halo.at[1], edges + 1, before)
     for step in range(1, groups):
@@ -273,13 +315,18 @@
     to_core, to_chip, to_s, to_t = (link.take(count) for count in (1, 1, ranks, groups))
     high = place.t // 2
 
-    def columns(index, size):
-        return pl.ds(pl.multiple_of(index * size, size), size)
-
     link.start(partial.at[:, columns(1 - place.core, 2 * width)], from_core, to_core, place.sibling)
     first, second, third = total_of(place, link, loss, stage_t, stage_s)
     first()
-    gather = Gather(place, link, slopes, lambda j: slopes_all.at[j])
+    chunks = 3
+    part = slopes.shape[1] // chunks
+    gather = Gather(
+        place,
+        link,
+        lambda q: slopes.at[:, pl.ds(q * part, part)],
+        lambda j, q: slopes_all.at[j, :, pl.ds(q * part, part)],
+        chunks,
+    )
     gather.start()
     link.arrived(from_core, to_core, place.sibling)
     mine = columns(place.core, 2 * width)
@@ -290,8 +337,9 @@
         from_core[span] = from_core[span] + partial[span, mine]
 
     link.start(from_core.at[:, columns(1 - high, width)], from_chip, to_chip, place.across)
+    gather.forward(0)
     second()
-    loss_total[...] = third()
+    gather.forward(1)
     link.arrived(from_chip, to_chip, place.across)
     kept = columns(high, width)
 
@@ -304,7 +352,8 @@
         taker = place.later(step)
         span = pl.ds(pl.multiple_of(taker * rows, rows), rows)
         link.start(from_chip.at[span], pieces.at[place.s], to_s + step, {"seq": taker})
-    gather.forward()
+    gather.forward(2)
+    gather.collect(0)
     own = pl.ds(pl.multiple_of(place.s * rows, rows), rows)
     pieces[place.s] = from_chip[own]
     for step in range(1, ranks):
@@ -321,7 +370,9 @@
             to_t + step,
             {"teacher": (place.t + step) % groups},
         )
-    gather.collect()
+    gather.collect(1)
+    gather.collect(2)
+    loss_total[...] = third()
     for step in range(1, groups):
         giver = (place.t + groups - step) % groups
         link.arrived(shares.at[(giver % 2) * 2 + giver // 2], to_t + step, place.sibling)
@@ -410,12 +461,17 @@
             jnp.zeros((6, channels), f32),
         ]
     )
-    proj_full, totals = exchange(
+    proj_full, dilated_all, totals = exchange(
         projection_kernel, 0, groups, ranks,
-        (projection[0], stats), [HBM, VMEM],
-        [((ranks, features, channels), bf16), ((8, channels), f32)], [HBM, VMEM],
+        (projection[0], dilated_weight.transpose(1, 0, 2), stats), [HBM, HBM, VMEM],
+        [
+            ((ranks, features, channels), bf16),
+            ((3, ranks, panel, branch), bf16),
+            ((8, channels), f32),
+        ],
+        [HBM, HBM, VMEM],
         [((groups, 8, channels), f32), ((ranks, 8, channels), f32)],
-        2 * ranks + groups, 1,
+        11 * ranks + groups, 2,
     )
     channel_mean = totals[0] / total_rows
     channel_var = totals[1] / total_rows - channel_mean * channel_mean
@@ -429,26 +485,24 @@
         preferred_element_type=f32,
     ).astype(bf16)
 
-    terms_all, dilated_all, pointwise_all, panels_all, halo = exchange(
+    terms_all, pointwise_all, panels_all, halo = exchange(
         forward_kernel, 1, groups, ranks,
         (
             terms.reshape(groups, rows, channels),
-            dilated_weight.transpose(1, 0, 2),
             pointwise_weight,
             panels,
             hidden_3d,
         ),
-        [HBM] * 5,
+        [HBM] * 4,
         [
             ((groups, rows, channels), bf16),
-            ((3, ranks, panel, branch), bf16),
             ((ranks,) + pointwise_weight.shape, bf16),
             ((ranks, rows, panel), bf16),
             ((2, win_grp, TAP_DILATION, channels), bf16),
         ],
-        [HBM] * 5,
+        [HBM] * 4,
         [],
-        5 * ranks + groups + 2, 4,
+        3 * ranks + groups + 2, 3,
     )
     target = terms_all[0].astype(f32)
     for group in range(1, groups):
@@ -458,12 +512,14 @@
     low = jnp.where(rank > 0, halo[0], jnp.zeros_like(halo[0]))
     high = jnp.where(rank < ranks - 1, halo[1], jnp.zeros_like(halo[1]))
     padded = jnp.concatenate([low, hidden_3d, high], axis=1)
-    preact = jnp.zeros((rows, branch), f32)
-    for tap in range(3):
-        shifted = padded[:, tap * TAP_DILATION : tap * TAP_DILATION + bins].reshape(rows, channels)
-        preact = preact + jnp.dot(
-            shifted, dilated_all[tap].reshape(channels, branch), preferred_element_type=f32
-        )
+    shifted = jnp.concatenate(
+        [padded[:, tap * TAP_DILATION : tap * TAP_DILATION + bins] for tap in range(3)], axis=2
+    )
+    preact = jnp.dot(
+        shifted.reshape(rows, 3 * channels),
+        dilated_all.reshape(3 * channels, branch),
+        preferred_element_type=f32,
+    )
     activated = gelu_tanh(preact).astype(bf16)
     pointwise_full = pointwise_all.reshape(branch, channels)
     student = inputs_f + jnp.dot(activated, pointwise_full, preferred_element_type=f32)
@@ -493,7 +549,7 @@
             ((groups, 8, 128), f32),
             ((ranks, 8, 128), f32),
         ],
-        3 * ranks + 2 * groups + 2, 1,
+        5 * ranks + 2 * groups + 2, 1,
     )
     loss_mean = 0.5 * loss_total[0, 0] / (channels * total_rows)
     pointwise_grad = shares.transpose(1, 0, 2).reshape(branch // ranks, channels)

time: 366 us -> 307 us (0.84)
  Pallas kernels: 317 us -> 265 us
  local copies, waits for them, and re-layouts: 19.2 us -> 12.5 us
    pallas_call x4, Pallas kernels: 317 us -> 265 us  [exchange(): pl.pallas_call(functools.partial(kernel, groups, ranks), out_shape=[jax.S...]
    slice x1 -> x0, local copies, waits for them, and re-layouts: 6.91 us -> none  [shards(): dilated_all[tap].reshape(channels, branch)]
    unnamed x32 -> x28, local copies, waits for them, and re-layouts: 9.47 us -> 9.67 us
where the time goes in v2:
time: 307 us; the launch traced here: 306 us
  Pallas kernels  265 us (86%)
  matrix products  22 us (7%)
  local copies, waits for them, and re-layouts  12.5 us (4%)
  other arithmetic  3.63 us (1%)
    pallas_call x4, Pallas kernels, exchange(): pl.pallas_call(functools.partial(kernel, groups, ranks), out_shape=[jax.S...  265 us
    unnamed x28, local copies, waits for them, and re-layouts  9.67 us
    dot_general x1, matrix products, shards(): jnp.dot(teacher_maps[0].reshape(groups * rows, -1), proj_full.reshape(ran...  6.5 us

profile of v2, /device:TPU:11, one launch (start us, length us, event | category | flops | bytes accessed | tf_op | source)
XLA Modules:
  0.0 306.3 jit_solution(4525230586700579597)
XLA Ops:
  0.6 1.6 convert_reduce_fusion
  2.4 1.2 copy-done
  3.6 1.1 copy-done.1
  4.6 106.8 %shard_map.76 = (bf16[8,192,1536]{2,1,0:T(8,128)(2,1)S(1)}, bf16[3,8,192,768]{3,2,1,0:T(8,128)(2,1)S(1)}, f32[8,1536]{1,0:T(8,128)S(1)}) custom-call(bf16[192,1536]{1,0:T(8,128)(2,1)S(1)} %bitcast.112, bf16[3,192,768]{2,1,0:T(8,128)(2,1)S(1)} %bitcast.110, f32[8,1536]{1,0:T(8,128)S(1)} %maximum_maximum_fusion.stats), custom_call_target="tpu_custom_call" | custom-call | tf_op jit(solution)/shard_map/pallas_call | solution.py:413
  111.6 0.8 fusion.13
  112.9 0.8 fusion.18.hidden
  113.7 0.8 copy-done.3
  114.5 1.5 copy-done.9
  116.1 6.5 %convolution_convert_fusion = bf16[1536,1280]{0,1:T(8,128)(2,1)S(1)} fusion(bf16[1280,1536]{1,0:T(8,128)(2,1)S(1)} %bitcast.126, bf16[1536,1536]{1,0:T(8,128)(2,1)S(1)} %bitcast.114), kind=kOutput, calls=%fused_computation | convolution fusion | flops 6041763840 | bytes 12582912 | tf_op jit(solution)/shard_map/dot_general | solution.py:482
  122.6 50.9 %shard_map.77 = (bf16[4,320,1536]{2,1,0:T(8,128)(2,1)S(1)}, bf16[8,96,1536]{2,1,0:T(8,128)(2,1)S(1)}, bf16[8,320,192]{2,1,0:T(8,128)(2,1)S(1)}, bf16[2,5,16,1536]{3,2,1,0:T(8,128)(2,1)S(1)}) custom-call(bf16[4,320,1536]{2,1,0:T(8,128)(2,1)S(1)} %bitcast.107, bf16[96,1536]{1,0:T(8,128)(2,1)S(1)} %copy-done.2, bf16[8,320,192]{2,1,0:T(8,128)(2,1)S(1)} %fusion.37.panels, ...), custom_call_target="tpu_custom_call" | custom-call | tf_op jit(solution)/shard_map/pallas_call | solution.py:413
  173.5 2.0 copy-done.4
  175.5 1.5 copy-done.5
  177.3 5.6 %fusion.2 = f32[320,768]{1,0:T(8,128)S(1)} fusion(bf16[4608,768]{1,0:T(8,128)(2,1)} %bitcast.113, bf16[320,1536]{1,0:T(8,128)(2,1)S(1)} %bitcast.124, bf16[320,1536]{1,0:T(8,128)(2,1)S(1)} %bitcast.103, bf16[320,1536]{1,0:T(8,128)(2,1)S(1)} %bitcast.123), kind=kOutput, calls=%fused_computation.3 | convolution fusion | flops 2273771520 | bytes 11010048 | tf_op jit(solution)/shard_map/dot_general | solution.py:518
  182.9 4.1 %multiply_reduce_fusion = (f32[]{:T(128)}, f32[320,1536]{1,0:T(8,128)S(1)}) fusion(bf16[4,320,1536]{2,1,0:T(8,128)(2,1)} %copy-done.4, bf16[768,1536]{1,0:T(8,128)(2,1)S(1)} %bitcast.115, f32[320,768]{1,0:T(8,128)S(1)} %fusion.2, bf16[320,1536]{1,0:T(8,128)(2,1)S(1)} %bitcast.117), kind=kOutput, calls=%fused_computation.32 | convolution fusion | flops 763576320 | bytes 10223620 | tf_op jit(solution)/shard_map/dot_general | solution.py:525
  187.0 1.6 fusion.36.partial
  188.6 1.3 fusion.25.slopes
  189.9 0.6 broadcast_in_dim.17.loss
  190.5 82.8 %shard_map.78 = (bf16[8,320,768]{2,1,0:T(8,128)(2,1)S(1)}, f32[4,96,384]{2,1,0:T(8,128)S(1)}, f32[8,128]{1,0:T(8,128)S(1)}) custom-call(bf16[320,768]{1,0:T(8,128)(2,1)S(1)} %fusion.25.slopes, f32[768,1536]{1,0:T(8,128)S(1)} %fusion.36.partial, f32[8,128]{1,0:T(8,128)S(1)} %broadcast_in_dim.17.loss), custom_call_target="tpu_custom_call" | custom-call | tf_op jit(solution)/shard_map/pallas_call | solution.py:413
  273.9 1.0 convolution_bitcast_fusion.1
  274.9 1.0 fusion.26
  275.9 1.0 convolution_bitcast_fusion
  277.0 24.9 %shard_map.79 = f32[3,192,768]{2,1,0:T(8,128)S(1)} custom-call(f32[3,192,768]{2,1,0:T(8,128)S(1)} %pad_maximum_fusion.partial), custom_call_target="tpu_custom_call" | custom-call | tf_op jit(solution)/shard_map/pallas_call | solution.py:413
  301.9 0.9 copy.14
  303.9 1.2 copy.31
  (35 shorter events, 2.2 us)
Async XLA Ops:
  0.6 110.9 %copy-start.7 = (bf16[5,64,1536]{2,1,0:T(8,128)(2,1)S(1)}, bf16[5,64,1536]{2,1,0:T(8,128)(2,1)}, u32[]{:S(2)}) copy-start(bf16[5,64,1536]{2,1,0:T(8,128)(2,1)} %param.5) | copy-start | bytes 2949124
  2.4 1.2 copy-start
  3.6 1.1 copy-start.1
  111.5 3.1 copy-start.3
  112.5 3.6 %copy-start.9 = (bf16[1,20,64,1536]{3,2,1,0:T(8,128)(2,1)S(1)}, bf16[1,20,64,1536]{3,2,1,0:T(8,128)(2,1)}, u32[]{:S(2)}) copy-start(bf16[1,20,64,1536]{3,2,1,0:T(8,128)(2,1)} %param.6) | copy-start | bytes 11796484
  116.1 6.5 %copy-start.2 = (bf16[96,1536]{1,0:T(8,128)(2,1)S(1)}, bf16[96,1536]{1,0:T(8,128)(2,1)}, u32[]{:S(2)}) copy-start(bf16[96,1536]{1,0:T(8,128)(2,1)} %pointwise.1) | copy-start | bytes 884740
  173.5 2.0 copy-start.4
  175.5 1.5 copy-start.5
  177.2 5.6 %copy-start.6 = (bf16[8,96,1536]{2,1,0:T(8,128)(2,1)S(1)}, bf16[8,96,1536]{2,1,0:T(8,128)(2,1)}, u32[]{:S(2)}) copy-start(bf16[8,96,1536]{2,1,0:T(8,128)(2,1)} %copy-done.5) | copy-start | bytes 7077892
  177.2 5.6 %copy-start.8 = (bf16[5,64,1536]{2,1,0:T(8,128)(2,1)S(1)}, bf16[5,64,1536]{2,1,0:T(8,128)(2,1)}, u32[]{:S(2)}) copy-start(bf16[5,64,1536]{2,1,0:T(8,128)(2,1)} %param.5) | copy-start | bytes 2949124

commit v3 on v2

--- a/solution.py
+++ b/solution.py
@@ -177,7 +177,7 @@
     stage_t, stage_s, send, recv, local,
 ):
     place, link = Place(groups, ranks), Link(send, recv)
-    chunks = 4
+    chunks = 6
     width = proj.shape[1] // chunks
     half = dilated.shape[2] // 2
     high = place.t // 2
@@ -227,7 +227,8 @@
         gather.forward(chunk)
     for chunk in range(2):
         gather_d.collect(chunk)
-        gather.forward(2 + chunk)
+        gather.forward(2 + 2 * chunk)
+        gather.forward(3 + 2 * chunk)
     for index in range(1, ranks):
         shard = gather_d.shard(index)
         link.arrived(dilated_all.at[taps[2], shard, :, mine], across + index, place.across)
@@ -249,16 +250,20 @@
     terms_all, pointwise_all, panels_all, halo, send, recv, local,
 ):
     place, link = Place(groups, ranks), Link(send, recv)
-    half = pointwise.shape[1] // 2
+    chunks = 2
+    part = pointwise.shape[1] // (2 * chunks)
     bins = hidden.shape[1]
     place.barrier()
-    mine, other = columns(place.core, half), columns(1 - place.core, half)
-    to_t, to_s, edges, side = (link.take(count) for count in (groups, ranks, 2, ranks))
+    to_t, to_s, edges = (link.take(count) for count in (groups, ranks, 2))
+    side = [link.take(ranks) for _ in range(chunks)]
     after, before = {"seq": place.later(1)}, {"seq": place.earlier(1)}
 
+    def part_of(core, chunk):
+        return columns(core * chunks + chunk, part)
+
     def spread(shard, chunk, index):
-        ref = pointwise_all.at[shard, :, mine]
-        link.start(ref, ref, side + index, place.sibling)
+        ref = pointwise_all.at[shard, :, part_of(place.core, chunk)]
+        link.start(ref, ref, side[chunk] + index, place.sibling)
 
     for step in range(1, groups):
         taker = (place.t + step) % groups
@@ -266,9 +271,9 @@
     gather = Gather(
         place,
         link,
-        lambda q: pointwise.at[:, mine],
-        lambda j, q: pointwise_all.at[j, :, mine],
-        1,
+        lambda q: pointwise.at[:, part_of(place.core, q)],
+        lambda j, q: pointwise_all.at[j, :, part_of(place.core, q)],
+        chunks,
         spread,
     )
     gather.start()
@@ -284,11 +289,14 @@
     ]
     for keep in keeps:
         keep.start()
-    gather.forward(0)
-    gather.collect(0)
+    for chunk in range(chunks):
+        gather.forward(chunk)
+    for chunk in range(chunks):
+        gather.collect(chunk)
     for index in range(1, ranks):
-        ref = pointwise_all.at[gather.shard(index), :, other]
-        link.arrived(ref, side + index, place.sibling)
+        for chunk in range(chunks):
+            ref = pointwise_all.at[gather.shard(index), :, part_of(1 - place.core, chunk)]
+            link.arrived(ref, side[chunk] + index, place.sibling)
     link.arrived(halo.at[0], edges, after)
     link.arrived(halo.at[1], edges + 1, before)
     for step in range(1, groups):
@@ -303,8 +311,8 @@
 
 def backward_kernel(
     groups, ranks, slopes, partial, loss,
-    slopes_all, shares, loss_total,
-    from_core, from_chip, pieces, stage_t, stage_s, send, recv, local,
+    slopes_all, from_chip, loss_total,
+    from_core, stage_t, stage_s, send, recv, local,
 ):
     place, link = Place(groups, ranks), Link(send, recv)
     width = partial.shape[1] // groups
@@ -312,7 +320,7 @@
     place.barrier()
     keep = pltpu.make_async_copy(slopes, slopes_all.at[place.s], local.at[0])
     keep.start()
-    to_core, to_chip, to_s, to_t = (link.take(count) for count in (1, 1, ranks, groups))
+    to_core, to_chip = link.take(1), link.take(1)
     high = place.t // 2
 
     link.start(partial.at[:, columns(1 - place.core, 2 * width)], from_core, to_core, place.sibling)
@@ -348,61 +356,69 @@
         span = pl.ds(pl.multiple_of(rank * rows, rows), rows)
         from_chip[span] = from_chip[span] + from_core[span, kept]
 
+    gather.forward(2)
+    for chunk in range(chunks):
+        gather.collect(chunk)
+    loss_total[...] = third()
+    keep.wait()
+    link.drain()
+
+
+def share_kernel(
+    groups, ranks, partial, block, out, shares, from_core, from_chip, pieces, send, recv
+):
+    place, link = Place(groups, ranks), Link(send, recv)
+    taps, depth, branch = partial.shape
+    half, tall = branch // 2, depth // 2
+    rows, width = block.shape[0] // ranks, block.shape[1]
+    parts = [(tap, pl.ds(low, tall)) for tap in range(taps) for low in (0, tall)]
+    a, b, c = (link.take(len(parts)) for _ in range(3))
+    to_s, to_t = link.take(ranks), link.take(groups)
+    mine, other = columns(place.core, half), columns(1 - place.core, half)
+    place.barrier()
+    for at, (tap, span) in enumerate(parts):
+        link.start(
+            partial.at[tap, span, other], from_core.at[tap, span], a + at, place.sibling
+        )
     for step in range(1, ranks):
         taker = place.later(step)
         span = pl.ds(pl.multiple_of(taker * rows, rows), rows)
-        link.start(from_chip.at[span], pieces.at[place.s], to_s + step, {"seq": taker})
-    gather.forward(2)
-    gather.collect(0)
-    own = pl.ds(pl.multiple_of(place.s * rows, rows), rows)
-    pieces[place.s] = from_chip[own]
+        link.start(block.at[span], pieces.at[place.s], to_s + step, {"seq": taker})
+    for at, (tap, span) in enumerate(parts):
+        link.arrived(from_core.at[tap, span], a + at, place.sibling)
+        from_core[tap, span] = from_core[tap, span] + partial[tap, span, mine]
+        link.start(from_core.at[tap, span], from_chip.at[tap, span], b + at, place.across)
+    pieces[place.s] = block[pl.ds(pl.multiple_of(place.s * rows, rows), rows)]
+
+    def add_chip(at):
+        tap, span = parts[at]
+        link.arrived(from_chip.at[tap, span], b + at, place.across)
+        out[tap, span, mine] = from_chip[tap, span] + from_core[tap, span]
+        link.start(out.at[tap, span, mine], out.at[tap, span, mine], c + at, place.sibling)
+
+    for at in range(len(parts) - 1):
+        add_chip(at)
     for step in range(1, ranks):
         link.arrived(pieces.at[place.earlier(step)], to_s + step, place.partner)
     summed = pieces[0]
     for rank in range(1, ranks):
         summed = summed + pieces[rank]
-    slot = place.core * 2 + high
-    shares[slot] = summed
+    kept = columns(place.core * 2 + place.t // 2, width)
+    shares[:, kept] = summed
     for step in range(1, groups):
         link.start(
-            shares.at[slot],
-            shares.at[slot],
+            shares.at[:, kept],
+            shares.at[:, kept],
             to_t + step,
             {"teacher": (place.t + step) % groups},
         )
-    gather.collect(1)
-    gather.collect(2)
-    loss_total[...] = third()
+    add_chip(len(parts) - 1)
+    for at, (tap, span) in enumerate(parts):
+        link.arrived(out.at[tap, span, other], c + at, place.sibling)
     for step in range(1, groups):
         giver = (place.t + groups - step) % groups
-        link.arrived(shares.at[(giver % 2) * 2 + giver // 2], to_t + step, place.sibling)
-    keep.wait()
-    link.drain()
-
-
-def share_kernel(groups, ranks, partial, out, from_core, from_chip, send, recv):
-    place, link = Place(groups, ranks), Link(send, recv)
-    taps, rows, width = partial.shape
-    half = width // 2
-    place.barrier(seq=False)
-    a, b, c = link.take(taps), link.take(taps), link.take(taps)
-
-    def columns(core):
-        return pl.ds(pl.multiple_of(core * half, half), half)
-
-    mine, other = columns(place.core), columns(1 - place.core)
-    for tap in range(taps):
-        link.start(partial.at[tap, :, other], from_core.at[tap], a + tap, place.sibling)
-    for tap in range(taps):
-        link.arrived(from_core.at[tap], a + tap, place.sibling)
-        from_core[tap] = from_core[tap] + partial[tap, :, mine]
-        link.start(from_core.at[tap], from_chip.at[tap], b + tap, place.across)
-    for tap in range(taps):
-        link.arrived(from_chip.at[tap], b + tap, place.across)
-        out[tap, :, mine] = from_chip[tap] + from_core[tap]
-        link.start(out.at[tap, :, mine], out.at[tap, :, mine], c + tap, place.sibling)
-    for tap in range(taps):
-        link.arrived(out.at[tap, :, other], c + tap, place.sibling)
+        ref = shares.at[:, columns((giver % 2) * 2 + giver // 2, width)]
+        link.arrived(ref, to_t + step, place.sibling)
     link.drain()
 
 
@@ -471,7 +487,7 @@
         ],
         [HBM, HBM, VMEM],
         [((groups, 8, channels), f32), ((ranks, 8, channels), f32)],
-        11 * ranks + groups, 2,
+        13 * ranks + groups, 2,
     )
     channel_mean = totals[0] / total_rows
     channel_var = totals[1] / total_rows - channel_mean * channel_mean
@@ -502,7 +518,7 @@
         ],
         [HBM] * 4,
         [],
-        3 * ranks + groups + 2, 3,
+        5 * ranks + groups + 2, 3,
     )
     target = terms_all[0].astype(f32)
     for group in range(1, groups):
@@ -532,27 +548,24 @@
     preact_grad = (back_grad * gelu_slope(preact)).astype(bf16)
     pointwise_part = column_product(activated, out_grad)
 
-    slopes_all, shares, loss_total = exchange(
+    slopes_all, block, loss_total = exchange(
         backward_kernel, 2, groups, ranks,
         (preact_grad, pointwise_part, jnp.full((8, 128), squared, f32)),
         [HBM, VMEM, VMEM],
         [
             ((ranks, rows, branch), bf16),
-            ((groups, branch // ranks, channels // groups), f32),
+            ((branch, channels // groups), f32),
             ((8, 128), f32),
         ],
         [HBM, VMEM, VMEM],
         [
             ((branch, channels // 2), f32),
-            ((branch, channels // groups), f32),
-            ((ranks, branch // ranks, channels // groups), f32),
             ((groups, 8, 128), f32),
             ((ranks, 8, 128), f32),
         ],
-        5 * ranks + 2 * groups + 2, 1,
+        4 * ranks + groups + 2, 1,
     )
     loss_mean = 0.5 * loss_total[0, 0] / (channels * total_rows)
-    pointwise_grad = shares.transpose(1, 0, 2).reshape(branch // ranks, channels)
 
     def windows(blocks):
         return (
@@ -574,12 +587,16 @@
             for tap in range(3)
         ]
     )
-    (dilated_grad,) = exchange(
+    dilated_grad, pointwise_grad = exchange(
         share_kernel, 3, groups, ranks,
-        (partial,), [VMEM],
-        [((3, panel, branch), f32)], [VMEM],
-        [((3, panel, branch // 2), f32), ((3, panel, branch // 2), f32)],
-        9, 0,
+        (partial, block), [VMEM, VMEM],
+        [((3, panel, branch), f32), ((branch // ranks, channels), f32)], [VMEM, VMEM],
+        [
+            ((3, panel, branch // 2), f32),
+            ((3, panel, branch // 2), f32),
+            ((ranks, branch // ranks, channels // groups), f32),
+        ],
+        18 + ranks + groups, 0,
     )
     return (loss_mean, dilated_grad.transpose(1, 0, 2), pointwise_grad)
 

time: 307 us -> 289 us (0.941)
  Pallas kernels: 265 us -> 247 us
    pallas_call x4, Pallas kernels: 265 us -> 247 us  [exchange(): pl.pallas_call(functools.partial(kernel, groups, ranks), out_shape=[jax.S...]
    unnamed x28 -> x29, local copies, waits for them, and re-layouts: 9.67 us -> 11.9 us
where the time goes in v3:
time: 289 us
  Pallas kernels  247 us (85%)
  matrix products  22 us (8%)
  local copies, waits for them, and re-layouts  13.9 us (5%)
  other arithmetic  3.62 us (1%)
    pallas_call x4, Pallas kernels, exchange(): pl.pallas_call(functools.partial(kernel, groups, ranks), out_shape=[jax.S...  247 us
    unnamed x29, local copies, waits for them, and re-layouts  11.9 us
    dot_general x1, matrix products, shards(): jnp.dot(teacher_maps[0].reshape(groups * rows, -1), proj_full.reshape(ran...  6.5 us

profile of v3, /device:TPU:11, one launch (start us, length us, event | category | flops | bytes accessed | tf_op | source)
XLA Modules:
  0.0 288.9 jit_solution(7203631244213600408)
XLA Ops:
  0.6 1.6 convert_reduce_fusion
  2.4 1.2 copy-done
  3.6 1.1 copy-done.1
  4.6 102.5 %shard_map.76 = (bf16[8,192,1536]{2,1,0:T(8,128)(2,1)S(1)}, bf16[3,8,192,768]{3,2,1,0:T(8,128)(2,1)S(1)}, f32[8,1536]{1,0:T(8,128)S(1)}) custom-call(bf16[192,1536]{1,0:T(8,128)(2,1)S(1)} %bitcast.108, bf16[3,192,768]{2,1,0:T(8,128)(2,1)S(1)} %bitcast.107, f32[8,1536]{1,0:T(8,128)S(1)} %maximum_maximum_fusion.stats), custom_call_target="tpu_custom_call" | custom-call | tf_op jit(solution)/shard_map/pallas_call | solution.py:429
  107.1 2.9 %copy-done.3 = bf16[3,8,192,768]{3,2,1,0:T(8,128)(2,1)} copy-done((bf16[3,8,192,768]{3,2,1,0:T(8,128)(2,1)}, bf16[3,8,192,768]{3,2,1,0:T(8,128)(2,1)S(1)}, u32[]{:S(2)}) %copy-start.3) | copy-done | bytes 7077912
  110.1 0.8 fusion.13
  111.5 0.8 fusion.18.hidden
  112.3 0.9 copy-done.9
  113.1 6.5 %convolution_convert_fusion = bf16[1536,1280]{0,1:T(8,128)(2,1)S(1)} fusion(bf16[1280,1536]{1,0:T(8,128)(2,1)S(1)} %bitcast.121, bf16[1536,1536]{1,0:T(8,128)(2,1)S(1)} %bitcast.110), kind=kOutput, calls=%fused_computation | convolution fusion | flops 6041763840 | bytes 12582912 | tf_op jit(solution)/shard_map/dot_general | solution.py:498
  119.7 51.1 %shard_map.77 = (bf16[4,320,1536]{2,1,0:T(8,128)(2,1)S(1)}, bf16[8,96,1536]{2,1,0:T(8,128)(2,1)S(1)}, bf16[8,320,192]{2,1,0:T(8,128)(2,1)S(1)}, bf16[2,5,16,1536]{3,2,1,0:T(8,128)(2,1)S(1)}) custom-call(bf16[4,320,1536]{2,1,0:T(8,128)(2,1)S(1)} %bitcast.103, bf16[96,1536]{1,0:T(8,128)(2,1)S(1)} %copy-done.2, bf16[8,320,192]{2,1,0:T(8,128)(2,1)S(1)} %fusion.37.panels, ...), custom_call_target="tpu_custom_call" | custom-call | tf_op jit(solution)/shard_map/pallas_call | solution.py:429
  170.8 2.0 copy-done.4
  172.8 1.5 copy-done.5
  174.5 5.6 %fusion.2 = f32[320,768]{1,0:T(8,128)S(1)} fusion(bf16[4608,768]{1,0:T(8,128)(2,1)} %bitcast.109, bf16[320,1536]{1,0:T(8,128)(2,1)S(1)} %bitcast.120, bf16[320,1536]{1,0:T(8,128)(2,1)S(1)} %bitcast.100, bf16[320,1536]{1,0:T(8,128)(2,1)S(1)} %bitcast.119), kind=kOutput, calls=%fused_computation.3 | convolution fusion | flops 2273771520 | bytes 11010048 | tf_op jit(solution)/shard_map/dot_general | solution.py:534
  180.2 4.1 %multiply_reduce_fusion = (f32[]{:T(128)}, f32[320,1536]{1,0:T(8,128)S(1)}) fusion(bf16[4,320,1536]{2,1,0:T(8,128)(2,1)} %copy-done.4, bf16[768,1536]{1,0:T(8,128)(2,1)S(1)} %bitcast.111, f32[320,768]{1,0:T(8,128)S(1)} %fusion.2, bf16[320,1536]{1,0:T(8,128)(2,1)S(1)} %bitcast.113), kind=kOutput, calls=%fused_computation.32 | convolution fusion | flops 763576320 | bytes 10223620 | tf_op jit(solution)/shard_map/dot_general | solution.py:541
  184.3 1.6 fusion.36.partial
  185.9 1.3 fusion.25.slopes
  187.2 0.6 broadcast_in_dim.17.loss
  187.8 57.1 %shard_map.78 = (bf16[8,320,768]{2,1,0:T(8,128)(2,1)S(1)}, f32[768,384]{1,0:T(8,128)S(1)}, f32[8,128]{1,0:T(8,128)S(1)}) custom-call(bf16[320,768]{1,0:T(8,128)(2,1)S(1)} %fusion.25.slopes, f32[768,1536]{1,0:T(8,128)S(1)} %fusion.36.partial, f32[8,128]{1,0:T(8,128)S(1)} %broadcast_in_dim.17.loss), custom_call_target="tpu_custom_call" | custom-call | tf_op jit(solution)/shard_map/pallas_call | solution.py:429
  245.5 1.0 convolution_bitcast_fusion.1
  246.5 1.0 fusion.26
  247.5 1.0 convolution_bitcast_fusion
  248.6 36.0 %shard_map.79 = (f32[3,192,768]{2,1,0:T(8,128)S(1)}, f32[96,1536]{1,0:T(8,128)S(1)}) custom-call(f32[3,192,768]{2,1,0:T(8,128)S(1)} %pad_maximum_fusion.partial, f32[768,384]{1,0:T(8,128)S(1)} %get-tuple-element.24.block), custom_call_target="tpu_custom_call" | custom-call | tf_op jit(solution)/shard_map/pallas_call | solution.py:429
  285.7 1.2 copy.28
  287.0 0.8 copy.29
  (35 shorter events, 2.2 us)
Async XLA Ops:
  0.6 109.4 %copy-start.7 = (bf16[5,64,1536]{2,1,0:T(8,128)(2,1)S(1)}, bf16[5,64,1536]{2,1,0:T(8,128)(2,1)}, u32[]{:S(2)}) copy-start(bf16[5,64,1536]{2,1,0:T(8,128)(2,1)} %param.5) | copy-start | bytes 2949124
  2.4 1.2 copy-start
  3.6 1.1 copy-start.1
  107.1 2.9 %copy-start.3 = (bf16[3,8,192,768]{3,2,1,0:T(8,128)(2,1)}, bf16[3,8,192,768]{3,2,1,0:T(8,128)(2,1)S(1)}, u32[]{:S(2)}) copy-start(bf16[3,8,192,768]{3,2,1,0:T(8,128)(2,1)S(1)} %get-tuple-element.18) | copy-start | bytes 21233668
  111.0 2.1 copy-start.9
  113.1 6.5 %copy-start.2 = (bf16[96,1536]{1,0:T(8,128)(2,1)S(1)}, bf16[96,1536]{1,0:T(8,128)(2,1)}, u32[]{:S(2)}) copy-start(bf16[96,1536]{1,0:T(8,128)(2,1)} %pointwise.1) | copy-start | bytes 884740
  170.8 2.0 copy-start.4
  172.8 1.5 copy-start.5
  174.5 5.6 %copy-start.6 = (bf16[8,96,1536]{2,1,0:T(8,128)(2,1)S(1)}, bf16[8,96,1536]{2,1,0:T(8,128)(2,1)}, u32[]{:S(2)}) copy-start(bf16[8,96,1536]{2,1,0:T(8,128)(2,1)} %copy-done.5) | copy-start | bytes 7077892
  174.5 5.6 %copy-start.8 = (bf16[5,64,1536]{2,1,0:T(8,128)(2,1)S(1)}, bf16[5,64,1536]{2,1,0:T(8,128)(2,1)}, u32[]{:S(2)}) copy-start(bf16[5,64,1536]{2,1,0:T(8,128)(2,1)} %param.5) | copy-start | bytes 2949124

commit v4 on v3

--- a/solution.py
+++ b/solution.py
@@ -172,13 +172,17 @@
     return pl.ds(pl.multiple_of(index * size, size), size)
 
 
+def row_chunks(rows, most):
+    return max(count for count in range(1, most + 1) if rows % (16 * count) == 0)
+
+
 def projection_kernel(
     groups, ranks, proj, dilated, stats, full, dilated_all, totals,
     stage_t, stage_s, send, recv, local,
 ):
     place, link = Place(groups, ranks), Link(send, recv)
-    chunks = 6
-    width = proj.shape[1] // chunks
+    chunks = row_chunks(proj.shape[0], 6)
+    height = proj.shape[0] // chunks
     half = dilated.shape[2] // 2
     high = place.t // 2
     mine, other = columns(place.core, half), columns(1 - place.core, half)
@@ -206,8 +210,8 @@
     gather = Gather(
         place,
         link,
-        lambda q: proj.at[:, pl.ds(q * width, width)],
-        lambda j, q: full.at[j, :, pl.ds(q * width, width)],
+        lambda q: proj.at[pl.ds(q * height, height)],
+        lambda j, q: full.at[j, pl.ds(q * height, height)],
         chunks,
     )
     gather_d = Gather(
@@ -225,10 +229,10 @@
     for chunk in range(2):
         gather_d.forward(chunk)
         gather.forward(chunk)
-    for chunk in range(2):
-        gather_d.collect(chunk)
-        gather.forward(2 + 2 * chunk)
-        gather.forward(3 + 2 * chunk)
+    gather_d.collect(0)
+    for chunk in range(2, chunks):
+        gather.forward(chunk)
+    gather_d.collect(1)
     for index in range(1, ranks):
         shard = gather_d.shard(index)
         link.arrived(dilated_all.at[taps[2], shard, :, mine], across + index, place.across)
@@ -326,13 +330,13 @@
     link.start(partial.at[:, columns(1 - place.core, 2 * width)], from_core, to_core, place.sibling)
     first, second, third = total_of(place, link, loss, stage_t, stage_s)
     first()
-    chunks = 3
-    part = slopes.shape[1] // chunks
+    chunks = row_chunks(slopes.shape[0], 5)
+    part = slopes.shape[0] // chunks
     gather = Gather(
         place,
         link,
-        lambda q: slopes.at[:, pl.ds(q * part, part)],
-        lambda j, q: slopes_all.at[j, :, pl.ds(q * part, part)],
+        lambda q: slopes.at[pl.ds(q * part, part)],
+        lambda j, q: slopes_all.at[j, pl.ds(q * part, part)],
         chunks,
     )
     gather.start()
@@ -356,7 +360,8 @@
         span = pl.ds(pl.multiple_of(rank * rows, rows), rows)
         from_chip[span] = from_chip[span] + from_core[span, kept]
 
-    gather.forward(2)
+    for chunk in range(2, chunks):
+        gather.forward(chunk)
     for chunk in range(chunks):
         gather.collect(chunk)
     loss_total[...] = third()
@@ -563,7 +568,7 @@
             ((groups, 8, 128), f32),
             ((ranks, 8, 128), f32),
         ],
-        4 * ranks + groups + 2, 1,
+        6 * ranks + groups + 2, 1,
     )
     loss_mean = 0.5 * loss_total[0, 0] / (channels * total_rows)
 

time: 289 us -> 292 us (1.010)
  Pallas kernels: 247 us -> 250 us
where the time goes in v4:
time: 292 us
  Pallas kernels  250 us (86%)
  matrix products  22 us (8%)
  local copies, waits for them, and re-layouts  13.9 us (5%)
  other arithmetic  3.62 us (1%)
    pallas_call x4, Pallas kernels, exchange(): pl.pallas_call(functools.partial(kernel, groups, ranks), out_shape=[jax.S...  250 us
    unnamed x29, local copies, waits for them, and re-layouts  11.9 us
    dot_general x1, matrix products, shards(): jnp.dot(teacher_maps[0].reshape(groups * rows, -1), proj_full.reshape(ran...  6.5 us

profile of v4, /device:TPU:11, one launch (start us, length us, event | category | flops | bytes accessed | tf_op | source)
XLA Modules:
  0.0 291.8 jit_solution(15401477666462225439)
XLA Ops:
  0.6 1.6 convert_reduce_fusion
  2.4 1.2 copy-done
  3.6 1.1 copy-done.1
  4.6 102.5 %shard_map.76 = (bf16[8,192,1536]{2,1,0:T(8,128)(2,1)S(1)}, bf16[3,8,192,768]{3,2,1,0:T(8,128)(2,1)S(1)}, f32[8,1536]{1,0:T(8,128)S(1)}) custom-call(bf16[192,1536]{1,0:T(8,128)(2,1)S(1)} %bitcast.108, bf16[3,192,768]{2,1,0:T(8,128)(2,1)S(1)} %bitcast.107, f32[8,1536]{1,0:T(8,128)S(1)} %maximum_maximum_fusion.stats), custom_call_target="tpu_custom_call" | custom-call | tf_op jit(solution)/shard_map/pallas_call | solution.py:434
  107.1 2.9 copy-done.3
  110.1 0.8 fusion.13
  111.5 0.8 fusion.18.hidden
  112.3 0.9 copy-done.9
  113.1 6.5 %convolution_convert_fusion = bf16[1536,1280]{0,1:T(8,128)(2,1)S(1)} fusion(bf16[1280,1536]{1,0:T(8,128)(2,1)S(1)} %bitcast.121, bf16[1536,1536]{1,0:T(8,128)(2,1)S(1)} %bitcast.110), kind=kOutput, calls=%fused_computation | convolution fusion | flops 6041763840 | bytes 12582912 | tf_op jit(solution)/shard_map/dot_general | solution.py:503
  119.7 51.1 %shard_map.77 = (bf16[4,320,1536]{2,1,0:T(8,128)(2,1)S(1)}, bf16[8,96,1536]{2,1,0:T(8,128)(2,1)S(1)}, bf16[8,320,192]{2,1,0:T(8,128)(2,1)S(1)}, bf16[2,5,16,1536]{3,2,1,0:T(8,128)(2,1)S(1)}) custom-call(bf16[4,320,1536]{2,1,0:T(8,128)(2,1)S(1)} %bitcast.103, bf16[96,1536]{1,0:T(8,128)(2,1)S(1)} %copy-done.2, bf16[8,320,192]{2,1,0:T(8,128)(2,1)S(1)} %fusion.37.panels, ...), custom_call_target="tpu_custom_call" | custom-call | tf_op jit(solution)/shard_map/pallas_call | solution.py:434
  170.8 2.0 copy-done.4
  172.8 1.5 copy-done.5
  174.5 5.6 %fusion.2 = f32[320,768]{1,0:T(8,128)S(1)} fusion(bf16[4608,768]{1,0:T(8,128)(2,1)} %bitcast.109, bf16[320,1536]{1,0:T(8,128)(2,1)S(1)} %bitcast.120, bf16[320,1536]{1,0:T(8,128)(2,1)S(1)} %bitcast.100, bf16[320,1536]{1,0:T(8,128)(2,1)S(1)} %bitcast.119), kind=kOutput, calls=%fused_computation.3 | convolution fusion | flops 2273771520 | bytes 11010048 | tf_op jit(solution)/shard_map/dot_general | solution.py:539
  180.2 4.1 %multiply_reduce_fusion = (f32[]{:T(128)}, f32[320,1536]{1,0:T(8,128)S(1)}) fusion(bf16[4,320,1536]{2,1,0:T(8,128)(2,1)} %copy-done.4, bf16[768,1536]{1,0:T(8,128)(2,1)S(1)} %bitcast.111, f32[320,768]{1,0:T(8,128)S(1)} %fusion.2, bf16[320,1536]{1,0:T(8,128)(2,1)S(1)} %bitcast.113), kind=kOutput, calls=%fused_computation.32 | convolution fusion | flops 763576320 | bytes 10223620 | tf_op jit(solution)/shard_map/dot_general | solution.py:546
  184.3 1.6 fusion.36.partial
  185.9 1.3 fusion.25.slopes
  187.2 0.6 broadcast_in_dim.17.loss
  187.8 58.3 %shard_map.78 = (bf16[8,320,768]{2,1,0:T(8,128)(2,1)S(1)}, f32[768,384]{1,0:T(8,128)S(1)}, f32[8,128]{1,0:T(8,128)S(1)}) custom-call(bf16[320,768]{1,0:T(8,128)(2,1)S(1)} %fusion.25.slopes, f32[768,1536]{1,0:T(8,128)S(1)} %fusion.36.partial, f32[8,128]{1,0:T(8,128)S(1)} %broadcast_in_dim.17.loss), custom_call_target="tpu_custom_call" | custom-call | tf_op jit(solution)/shard_map/pallas_call | solution.py:434
  246.7 1.0 convolution_bitcast_fusion.1
  247.7 1.0 fusion.26
  248.7 1.0 convolution_bitcast_fusion
  249.8 37.7 %shard_map.79 = (f32[3,192,768]{2,1,0:T(8,128)S(1)}, f32[96,1536]{1,0:T(8,128)S(1)}) custom-call(f32[3,192,768]{2,1,0:T(8,128)S(1)} %pad_maximum_fusion.partial, f32[768,384]{1,0:T(8,128)S(1)} %get-tuple-element.24.block), custom_call_target="tpu_custom_call" | custom-call | tf_op jit(solution)/shard_map/pallas_call | solution.py:434
  288.6 1.2 copy.28
  289.8 0.8 copy.29
  (35 shorter events, 2.2 us)
Async XLA Ops:
  0.6 109.4 %copy-start.7 = (bf16[5,64,1536]{2,1,0:T(8,128)(2,1)S(1)}, bf16[5,64,1536]{2,1,0:T(8,128)(2,1)}, u32[]{:S(2)}) copy-start(bf16[5,64,1536]{2,1,0:T(8,128)(2,1)} %param.5) | copy-start | bytes 2949124
  2.4 1.2 copy-start
  3.6 1.1 copy-start.1
  107.1 2.9 %copy-start.3 = (bf16[3,8,192,768]{3,2,1,0:T(8,128)(2,1)}, bf16[3,8,192,768]{3,2,1,0:T(8,128)(2,1)S(1)}, u32[]{:S(2)}) copy-start(bf16[3,8,192,768]{3,2,1,0:T(8,128)(2,1)S(1)} %get-tuple-element.18) | copy-start | bytes 21233668
  111.0 2.1 copy-start.9
  113.1 6.5 %copy-start.2 = (bf16[96,1536]{1,0:T(8,128)(2,1)S(1)}, bf16[96,1536]{1,0:T(8,128)(2,1)}, u32[]{:S(2)}) copy-start(bf16[96,1536]{1,0:T(8,128)(2,1)} %pointwise.1) | copy-start | bytes 884740
  170.8 2.0 copy-start.4
  172.8 1.5 copy-start.5
  174.5 5.6 %copy-start.6 = (bf16[8,96,1536]{2,1,0:T(8,128)(2,1)S(1)}, bf16[8,96,1536]{2,1,0:T(8,128)(2,1)}, u32[]{:S(2)}) copy-start(bf16[8,96,1536]{2,1,0:T(8,128)(2,1)} %copy-done.5) | copy-start | bytes 7077892
  174.5 5.6 %copy-start.8 = (bf16[5,64,1536]{2,1,0:T(8,128)(2,1)S(1)}, bf16[5,64,1536]{2,1,0:T(8,128)(2,1)}, u32[]{:S(2)}) copy-start(bf16[5,64,1536]{2,1,0:T(8,128)(2,1)} %param.5) | copy-start | bytes 2949124
